TPU v7x, 32 devices: a whole 2x2x4 slice. The times are simulated.
32 devices in a mesh: gx: 4 (over y, core), gy: 8 (over z, x).
Axes of the slice: x: 2, y: 2, z: 4, core: 2. Of those that a mesh axis runs over, the one named last changes fastest.
Arguments:
- pressure: float32 [128, 256, 128], P('gx', 'gy'), may hold values from -6 to 6
- vel_x: float32 [128, 256, 128], P('gx', 'gy'), may hold values from -6 to 6
- vel_y: float32 [128, 256, 128], P('gx', 'gy'), may hold values from -6 to 6
- vel_z: float32 [128, 256, 128], P('gx', 'gy'), may hold values from -6 to 6
- material: int32 [128, 256, 128], P('gx', 'gy'), may hold values from 0 to 3
- density_table: float32 [4], replicated, may hold values from 0.5 to 4
- speed_table: float32 [4], replicated, may hold values from 0.3 to 1
- panel_vals: float32 [64, 128, 8, 128], P(('gx', 'gy')), may hold values from -6 to 6
- panel_tile: int32 [64, 128, 1], P(('gx', 'gy')), may hold values from 0 to 31; in each aligned block of 256 rows (0 to 255, 256 to 511, ..., all dimensions but the last counted through in order) at most 16 rows name the same one
- panel_cell: int32 [64, 128], P(('gx', 'gy')), may hold values from 0 to 1023
Outputs:
- pressure_out: float32 [128, 256, 128], P('gx', 'gy')
- vel_x_out: float32 [128, 256, 128], P('gx', 'gy')
- vel_y_out: float32 [128, 256, 128], P('gx', 'gy')
- vel_z_out: float32 [128, 256, 128], P('gx', 'gy')
Inputs may be any that keep to these rules, and one draw needn't show every extreme that they name: `panel_tile`: among the 256 columns of the panels of one device, no tile is named more than 16 times, a bound that some block reaches.
All inputs are finite; a program needn't handle non-finite values.
Results may differ from a plain program's by a relative error of at most 0.00002.
Values sent between devices are 32-bit elements; how exact they have to be, the bound alone decides.
A program may use at most 64 MiB of HBM per device.

v0:
```python
import jax
import jax.numpy as jnp
from jax import lax
from jax.sharding import PartitionSpec as P

courant = 0.55


def shifted(block, axis, distance):
    devices = range(lax.axis_size(axis))
    route = [(i - distance, i) for i in devices if i - distance in devices]
    return lax.ppermute(block, axis, route)


def lookup(material, table):
    total = jnp.zeros(material.shape, jnp.float32)
    for index in range(table.shape[0]):
        total = total + jnp.where(material == index, table[index], 0.0)
    return total


def per_device(
    pressure,
    vel_x,
    vel_y,
    vel_z,
    material,
    density_table,
    speed_table,
    panel_vals,
    panel_tile,
    panel_cell,
):
    size_x = lax.axis_size("gx")
    size_y = lax.axis_size("gy")
    devices = size_x * size_y
    cells_x, cells_y, layers = pressure.shape
    steps = panel_vals.shape[2]
    tile_cells = cells_x * cells_y
    density = lookup(material, density_table)
    speed = lookup(material, speed_table)
    buoyancy = 1.0 / density
    stiffness = density * speed * speed
    target = panel_tile.reshape(-1)
    columns = target.shape[0]
    slots = max(2, 2 * columns // devices)
    order = jnp.arange(columns, dtype=jnp.int32)
    earlier = (target[:, None] == target[None, :]) & (order[None, :] < order[:, None])
    position = target * slots + jnp.sum(earlier.astype(jnp.int32), axis=1)
    values = panel_vals.reshape(columns, steps, layers)
    outgoing = jnp.zeros((devices * slots, steps, layers), jnp.float32).at[position].set(values)
    outgoing = outgoing.reshape(size_x, size_y, slots, steps, layers)
    cell_floats = jnp.full((devices * slots,), float(tile_cells), jnp.float32)
    cell_floats = cell_floats.at[position].set(panel_cell.reshape(-1).astype(jnp.float32))
    cell_floats = cell_floats.reshape(size_x, size_y, slots)
    holder = {}
    incoming, arrived_cells = (
        lax.all_to_all(
            lax.all_to_all(outgoing, "gx", split_axis=0, concat_axis=0, tiled=True),
            "gy",
            split_axis=1,
            concat_axis=1,
            tiled=True,
        ),
        lax.all_to_all(
            lax.all_to_all(cell_floats, "gx", split_axis=0, concat_axis=0, tiled=True),
            "gy",
            split_axis=1,
            concat_axis=1,
            tiled=True,
        ),
    )
    holder["incoming"] = incoming.reshape(devices * slots, steps, layers)
    holder["cells"] = arrived_cells.reshape(-1).astype(jnp.int32)
    for step in range(steps):
        arriving = holder["incoming"][:, step, :]
        source = (
            jnp.zeros((tile_cells, layers), jnp.float32)
            .at[holder["cells"]]
            .add(arriving, mode="drop")
        )
        source = source.reshape(cells_x, cells_y, layers)
        upper_x = shifted(pressure[:1], "gx", -1)
        upper_y = shifted(pressure[:, :1], "gy", -1)
        next_x = jnp.concatenate([pressure[1:], upper_x], axis=0)
        next_y = jnp.concatenate([pressure[:, 1:], upper_y], axis=1)
        next_z = jnp.concatenate([pressure[:, :, 1:], jnp.zeros_like(pressure[:, :, :1])], axis=2)
        vel_x = vel_x - courant * buoyancy * (next_x - pressure)
        vel_y = vel_y - courant * buoyancy * (next_y - pressure)
        vel_z = vel_z - courant * buoyancy * (next_z - pressure)
        lower_x = shifted(vel_x[-1:], "gx", 1)
        lower_y = shifted(vel_y[:, -1:], "gy", 1)
        prev_x = jnp.concatenate([lower_x, vel_x[:-1]], axis=0)
        prev_y = jnp.concatenate([lower_y, vel_y[:, :-1]], axis=1)
        prev_z = jnp.concatenate([jnp.zeros_like(vel_z[:, :, :1]), vel_z[:, :, :-1]], axis=2)
        divergence = vel_x - prev_x + (vel_y - prev_y)
        divergence = divergence + (vel_z - prev_z)
        pressure = pressure - courant * stiffness * divergence + courant * stiffness * source
    return (pressure, vel_x, vel_y, vel_z)


def solution(mesh):
    return jax.shard_map(
        per_device,
        mesh=mesh,
        in_specs=(
            P("gx", "gy", None),
            P("gx", "gy", None),
            P("gx", "gy", None),
            P("gx", "gy", None),
            P("gx", "gy", None),
            P(),
            P(),
            P(("gx", "gy"), None, None, None),
            P(("gx", "gy"), None, None),
            P(("gx", "gy"), None),
        ),
        out_specs=(
            P("gx", "gy", None),
            P("gx", "gy", None),
            P("gx", "gy", None),
            P("gx", "gy", None),
        ),
        check_vma=False,
    )
```

profile of v0, /device:TPU:0, one launch (start us, length us, event | category | flops | bytes accessed | tf_op | source)
XLA Modules:
  0.0 355.8 jit_solution(2780622458270188160)
XLA Ops:
  5.1 4.2 %all-to-all-start = ((f32[4,1,128]{2,1,0:T(1,128)}), f32[4,1,128]{2,1,0:T(1,128)S(1)}, u32[]{:S(2)}, u32[]{:S(2)}) async-start(f32[4,1,128]{2,1,0:T(1,128)} %reshape.208), calls=%async_computation | async-start | bytes 4096 | tf_op jit(solution)/shard_map/all_to_all | solution.py:66
  10.9 24.0 %scatter_fusion = f32[512,8,128]{2,1,0:T(8,128)} fusion(f32[512,8,128]{2,1,0:T(8,128)} %broadcast_in_dim.64, s32[256]{0:T(256)S(1)} %bitcast.89, f32[256,8,128]{2,1,0:T(8,128)S(1)} %bitcast.78), kind=kCustom, calls=%fused_computation.1 | custom fusion | bytes 3146752 | tf_op jit(solution)/shard_map/scatter | solution.py:51
  34.8 3.6 %all-to-all-start.2 = ((f32[4,8,16,8,128]{4,3,2,1,0:T(8,128)}), f32[4,8,16,8,128]{4,3,2,1,0:T(8,128)S(1)}, u32[]{:S(2)}, u32[]{:S(2)}) async-start(f32[4,8,16,8,128]{4,3,2,1,0:T(8,128)} %bitcast.15), calls=%async_computation.2 | async-start | bytes 4194304 | tf_op jit(solution)/shard_map/all_to_all | solution.py:59
  40.3 23.8 %all-to-all-done.2 = f32[4,8,16,8,128]{4,3,2,1,0:T(8,128)S(1)} async-done(((f32[4,8,16,8,128]{4,3,2,1,0:T(8,128)}), f32[4,8,16,8,128]{4,3,2,1,0:T(8,128)S(1)}, u32[]{:S(2)}, u32[]{:S(2)}) %all-to-all-start.2) | async-done | bytes 2097184 | tf_op jit(solution)/shard_map/all_to_all | solution.py:59
  64.1 6.2 %all-to-all-start.1 = ((f32[4,8,16]{2,0,1:T(4,128)}), f32[4,8,16]{2,0,1:T(4,128)S(1)}, u32[]{:S(2)}, u32[]{:S(2)}) async-start(f32[4,8,16]{2,0,1:T(4,128)} %copy.35), calls=%async_computation.1 | async-start | bytes 32768 | tf_op jit(solution)/shard_map/all_to_all | solution.py:65
  71.8 5.1 %all-to-all-done.1 = f32[4,8,16]{2,0,1:T(4,128)S(1)} async-done(((f32[4,8,16]{2,0,1:T(4,128)}), f32[4,8,16]{2,0,1:T(4,128)S(1)}, u32[]{:S(2)}, u32[]{:S(2)}) %all-to-all-start.1) | async-done | bytes 2080 | tf_op jit(solution)/shard_map/all_to_all | solution.py:65
  76.9 4.3 %all-to-all-start.3 = ((f32[4,8,16,8,128]{4,3,2,0,1:T(8,128)}), f32[4,8,16,8,128]{4,3,2,0,1:T(8,128)}, u32[]{:S(2)}, u32[]{:S(2)}) async-start(f32[4,8,16,8,128]{4,3,2,0,1:T(8,128)} %copy.37), calls=%async_computation.3 | async-start | bytes 4194304 | tf_op jit(solution)/shard_map/all_to_all | solution.py:58
  89.6 3.2 collective-permute-done.2
  92.8 4.3 %fusion.9 = (f32[32,32,128]{2,1,0:T(8,128)S(1)}, f32[32,32,128]{2,1,0:T(8,128)S(1)}) fusion(f32[32,32,128]{2,1,0:T(8,128)} %param.12, f32[32,32,128]{2,1,0:T(8,128)S(1)} %copy-done, f32[32,1,128]{2,1,0:T(1,128)S(1)} %collective-permute-done.2, f32[32,31,128]{2,1,0:T(8,128)} %slice.300, pred[32,32,128]{2,1,0:T(8,128)(4,1)S(1)} %get-tuple-element.8, ...), kind=kLoop, calls=%fused_computation.23 | loop fusion | flops 2228224 | bytes 4194320 | tf_op jit(solution)/shard_map/sub | solution.py:89
  99.4 15.0 %collective-permute-start.3 = (f32[32,1,128]{2,1,0:T(1,128)S(1)}, f32[32,1,128]{2,1,0:T(1,128)S(1)}, u32[]{:S(2)}, u32[]{:S(2)}) collective-permute-start(f32[32,1,128]{2,1,0:T(1,128)S(1)} %slice.386), channel_id=1, source_target_pairs={{0,1},{1,2},{2,3},{3,4},{4,5},{5,6},{6,7},{8,9},{9,10},{10,11},{11... | collective-permute-start | bytes 49160 | tf_op jit(solution)/shard_map/ppermute | solution.py:12
  114.3 13.9 %all-to-all-done.3 = f32[4,8,16,8,128]{4,3,2,0,1:T(8,128)} async-done(((f32[4,8,16,8,128]{4,3,2,0,1:T(8,128)}), f32[4,8,16,8,128]{4,3,2,0,1:T(8,128)}, u32[]{:S(2)}, u32[]{:S(2)}) %all-to-all-start.3) | async-done | bytes 2097184 | tf_op jit(solution)/shard_map/all_to_all | solution.py:58
  135.6 6.9 %fusion.7 = f32[32,32,128]{2,1,0:T(8,128)S(1)} fusion(f32[32,32,128]{2,1,0:T(8,128)S(1)} %copy-done, f32[32,32,128]{2,1,0:T(8,128)S(1)} %get-tuple-element.39, f32[31,32,128]{2,1,0:T(8,128)} %slice.385, f32[1,32,128]{2,1,0:T(8,128)S(1)} %collective-permute-done.1, f32[32,32,128]{2,1,0:T(8,128)S(1)} %get-tuple-element.38, f32[32,31,128]{2,1,0:T(8,128)S(1)} %bitcast.53, ...), kind=kLoop, calls=%fused_computation.20 | loop fusion | flops 3670016 | bytes 5238816 | tf_op jit(solution)/shard_map/add | solution.py:98
  145.7 3.9 %collective-permute-done.6 = f32[32,1,128]{2,1,0:T(1,128)S(1)} collective-permute-done((f32[32,1,128]{2,1,0:T(1,128)S(1)}, f32[32,1,128]{2,1,0:T(1,128)S(1)}, u32[]{:S(2)}, u32[]{:S(2)}) %collective-permute-start.6) | collective-permute-done | bytes 16416 | tf_op jit(solution)/shard_map/ppermute | solution.py:12
  149.6 3.9 %multiply_subtract_fusion.6 = (f32[32,32,128]{2,1,0:T(8,128)}, f32[32,32,128]{2,1,0:T(8,128)S(1)}, f32[32,32,128]{2,1,0:T(8,128)S(1)}) fusion(f32[32,32,128]{2,1,0:T(8,128)S(1)} %get-tuple-element.4, f32[32,32,128]{2,1,0:T(8,128)S(1)} %fusion.7, f32[32,32,127]{2,1,0:T(8,128)S(1)} %slice.398, pred[32,32,128]{2,1,0:T(8,128)(4,1)S(1)} %get-tuple-element.8, ...), kind=kLoop, calls=%fused_computation.122 | loop fusion | flops 2621440 | bytes 5763088 | tf_op jit(solution)/shard_map/sub | solution.py:90
  156.4 12.8 %collective-permute-start.7 = (f32[32,1,128]{2,1,0:T(1,128)S(1)}, f32[32,1,128]{2,1,0:T(1,128)S(1)}, u32[]{:S(2)}, u32[]{:S(2)}) collective-permute-start(f32[32,1,128]{2,1,0:T(1,128)S(1)} %slice.396), channel_id=1, source_target_pairs={{0,1},{1,2},{2,3},{3,4},{4,5},{5,6},{6,7},{8,9},{9,10},{10,11},{11... | collective-permute-start | bytes 49160 | tf_op jit(solution)/shard_map/ppermute | solution.py:12
  173.2 7.1 %fusion.16 = f32[32,32,128]{2,1,0:T(8,128)S(1)} fusion(f32[32,32,128]{2,1,0:T(8,128)S(1)} %fusion.7, f32[32,32,128]{2,1,0:T(8,128)} %copy-done.5, f32[31,32,128]{2,1,0:T(8,128)S(1)} %slice.393, f32[1,32,128]{2,1,0:T(8,128)S(1)} %collective-permute-done.5, f32[32,32,128]{2,1,0:T(8,128)S(1)} %get-tuple-element.36, f32[32,31,128]{2,1,0:T(8,128)S(1)} %bitcast.54, ...), kind=kLoop, calls=%fused_computation.33 | loop fusion | flops 3670016 | bytes 5238816 | tf_op jit(solution)/shard_map/add | solution.py:98
  189.8 4.6 %collective-permute-start.11 = (f32[32,1,128]{2,1,0:T(1,128)S(1)}, f32[32,1,128]{2,1,0:T(1,128)S(1)}, u32[]{:S(2)}, u32[]{:S(2)}) collective-permute-start(f32[32,1,128]{2,1,0:T(1,128)S(1)} %slice.407), channel_id=1, source_target_pairs={{0,1},{1,2},{2,3},{3,4},{4,5},{5,6},{6,7},{8,9},{9,10},{10,11},{11... | collective-permute-start | bytes 49160 | tf_op jit(solution)/shard_map/ppermute | solution.py:12
  194.4 4.1 %collective-permute-start.9 = (f32[1,32,128]{2,1,0:T(8,128)S(1)}, f32[1,32,128]{2,1,0:T(8,128)S(1)}, u32[]{:S(2)}, u32[]{:S(2)}) collective-permute-start(f32[1,32,128]{2,1,0:T(8,128)S(1)} %slice.403), channel_id=1, source_target_pairs={{0,8},{8,16},{16,24},{1,9},{9,17},{17,25},{2,10},{10,18},{18,26},{... | collective-permute-start | bytes 49160 | tf_op jit(solution)/shard_map/ppermute | solution.py:12
  202.4 6.7 %fusion.25 = f32[32,32,128]{2,1,0:T(8,128)S(1)} fusion(f32[32,32,128]{2,1,0:T(8,128)S(1)} %fusion.16, f32[32,32,128]{2,1,0:T(8,128)} %copy-done.7, f32[31,32,128]{2,1,0:T(8,128)S(1)} %slice.404, f32[1,32,128]{2,1,0:T(8,128)S(1)} %collective-permute-done.9, f32[32,32,128]{2,1,0:T(8,128)S(1)} %get-tuple-element.33, f32[32,31,128]{2,1,0:T(8,128)S(1)} %bitcast.55, ...), kind=kLoop, calls=%fused_computation.46 | loop fusion | flops 3670016 | bytes 5238816 | tf_op jit(solution)/shard_map/add | solution.py:98
  212.4 4.5 %collective-permute-done.14 = f32[32,1,128]{2,1,0:T(1,128)S(1)} collective-permute-done((f32[32,1,128]{2,1,0:T(1,128)S(1)}, f32[32,1,128]{2,1,0:T(1,128)S(1)}, u32[]{:S(2)}, u32[]{:S(2)}) %collective-permute-start.14) | collective-permute-done | bytes 16416 | tf_op jit(solution)/shard_map/ppermute | solution.py:12
  216.8 3.9 %multiply_subtract_fusion.4 = (f32[32,32,128]{2,1,0:T(8,128)}, f32[32,32,128]{2,1,0:T(8,128)S(1)}, f32[32,32,128]{2,1,0:T(8,128)S(1)}) fusion(f32[32,32,128]{2,1,0:T(8,128)S(1)} %get-tuple-element.32, f32[32,32,128]{2,1,0:T(8,128)S(1)} %fusion.25, f32[32,32,127]{2,1,0:T(8,128)S(1)} %slice.420, pred[32,32,128]{2,1,0:T(8,128)(4,1)S(1)} %get-tuple-element.8, ...), kind=kLoop, calls=%fused_computation.120 | loop fusion | flops 2621440 | bytes 5763088 | tf_op jit(solution)/shard_map/sub | solution.py:90
  223.7 4.7 %collective-permute-start.15 = (f32[32,1,128]{2,1,0:T(1,128)S(1)}, f32[32,1,128]{2,1,0:T(1,128)S(1)}, u32[]{:S(2)}, u32[]{:S(2)}) collective-permute-start(f32[32,1,128]{2,1,0:T(1,128)S(1)} %slice.418), channel_id=1, source_target_pairs={{0,1},{1,2},{2,3},{3,4},{4,5},{5,6},{6,7},{8,9},{9,10},{10,11},{11... | collective-permute-start | bytes 49160 | tf_op jit(solution)/shard_map/ppermute | solution.py:12
  232.3 7.1 %fusion.34 = f32[32,32,128]{2,1,0:T(8,128)S(1)} fusion(f32[32,32,128]{2,1,0:T(8,128)S(1)} %fusion.25, f32[32,32,128]{2,1,0:T(8,128)} %copy-done.9, f32[31,32,128]{2,1,0:T(8,128)S(1)} %slice.415, f32[1,32,128]{2,1,0:T(8,128)S(1)} %collective-permute-done.13, f32[32,32,128]{2,1,0:T(8,128)S(1)} %get-tuple-element.30, f32[32,31,128]{2,1,0:T(8,128)S(1)} %bitcast.56, ...), kind=kLoop, calls=%fused_computation.59 | loop fusion | flops 3670016 | bytes 5238816 | tf_op jit(solution)/shard_map/add | solution.py:98
  250.5 3.6 %collective-permute-start.17 = (f32[1,32,128]{2,1,0:T(8,128)S(1)}, f32[1,32,128]{2,1,0:T(8,128)S(1)}, u32[]{:S(2)}, u32[]{:S(2)}) collective-permute-start(f32[1,32,128]{2,1,0:T(8,128)S(1)} %slice.425), channel_id=1, source_target_pairs={{0,8},{8,16},{16,24},{1,9},{9,17},{17,25},{2,10},{10,18},{18,26},{... | collective-permute-start | bytes 49160 | tf_op jit(solution)/shard_map/ppermute | solution.py:12
  261.3 6.7 %fusion.43 = f32[32,32,128]{2,1,0:T(8,128)S(1)} fusion(f32[32,32,128]{2,1,0:T(8,128)S(1)} %fusion.34, f32[32,32,128]{2,1,0:T(8,128)} %copy-done.11, f32[31,32,128]{2,1,0:T(8,128)S(1)} %slice.426, f32[1,32,128]{2,1,0:T(8,128)S(1)} %collective-permute-done.17, f32[32,32,128]{2,1,0:T(8,128)S(1)} %get-tuple-element.27, f32[32,31,128]{2,1,0:T(8,128)S(1)} %bitcast.57, ...), kind=kLoop, calls=%fused_computation.72 | loop fusion | flops 3670016 | bytes 5238816 | tf_op jit(solution)/shard_map/add | solution.py:98
  279.1 4.0 %collective-permute-start.21 = (f32[1,32,128]{2,1,0:T(8,128)S(1)}, f32[1,32,128]{2,1,0:T(8,128)S(1)}, u32[]{:S(2)}, u32[]{:S(2)}) collective-permute-start(f32[1,32,128]{2,1,0:T(8,128)S(1)} %slice.436), channel_id=1, source_target_pairs={{0,8},{8,16},{16,24},{1,9},{9,17},{17,25},{2,10},{10,18},{18,26},{... | collective-permute-start | bytes 49160 | tf_op jit(solution)/shard_map/ppermute | solution.py:12
  290.1 6.7 %fusion.52 = f32[32,32,128]{2,1,0:T(8,128)S(1)} fusion(f32[32,32,128]{2,1,0:T(8,128)S(1)} %fusion.43, f32[32,32,128]{2,1,0:T(8,128)} %copy-done.13, f32[31,32,128]{2,1,0:T(8,128)S(1)} %slice.437, f32[1,32,128]{2,1,0:T(8,128)S(1)} %collective-permute-done.21, f32[32,32,128]{2,1,0:T(8,128)S(1)} %get-tuple-element.24, f32[32,31,128]{2,1,0:T(8,128)S(1)} %bitcast.58, ...), kind=kLoop, calls=%fused_computation.85 | loop fusion | flops 3670016 | bytes 5238816 | tf_op jit(solution)/shard_map/add | solution.py:98
  307.9 4.0 %collective-permute-start.25 = (f32[1,32,128]{2,1,0:T(8,128)S(1)}, f32[1,32,128]{2,1,0:T(8,128)S(1)}, u32[]{:S(2)}, u32[]{:S(2)}) collective-permute-start(f32[1,32,128]{2,1,0:T(8,128)S(1)} %slice.447), channel_id=1, source_target_pairs={{0,8},{8,16},{16,24},{1,9},{9,17},{17,25},{2,10},{10,18},{18,26},{... | collective-permute-start | bytes 49160 | tf_op jit(solution)/shard_map/ppermute | solution.py:12
  318.9 6.7 %fusion.61 = f32[32,32,128]{2,1,0:T(8,128)S(1)} fusion(f32[32,32,128]{2,1,0:T(8,128)S(1)} %fusion.52, f32[32,32,128]{2,1,0:T(8,128)} %copy-done.15, f32[31,32,128]{2,1,0:T(8,128)S(1)} %slice.448, f32[1,32,128]{2,1,0:T(8,128)S(1)} %collective-permute-done.25, f32[32,32,128]{2,1,0:T(8,128)S(1)} %get-tuple-element.21, f32[32,31,128]{2,1,0:T(8,128)S(1)} %bitcast.59, ...), kind=kLoop, calls=%fused_computation.98 | loop fusion | flops 3670016 | bytes 5238816 | tf_op jit(solution)/shard_map/add | solution.py:98
  332.7 3.9 %multiply_subtract_fusion = (f32[32,32,128]{2,1,0:T(8,128)}, f32[32,32,128]{2,1,0:T(8,128)S(1)}, f32[32,32,128]{2,1,0:T(8,128)S(1)}) fusion(f32[32,32,128]{2,1,0:T(8,128)S(1)} %get-tuple-element.20, f32[32,32,128]{2,1,0:T(8,128)S(1)} %fusion.61, f32[32,32,127]{2,1,0:T(8,128)S(1)} %slice.464, pred[32,32,128]{2,1,0:T(8,128)(4,1)S(1)} %get-tuple-element.8, ...), kind=kLoop, calls=%fused_computation.116 | loop fusion | flops 2621440 | bytes 5763088 | tf_op jit(solution)/shard_map/sub | solution.py:90
  337.4 4.0 %collective-permute-start.29 = (f32[1,32,128]{2,1,0:T(8,128)S(1)}, f32[1,32,128]{2,1,0:T(8,128)S(1)}, u32[]{:S(2)}, u32[]{:S(2)}) collective-permute-start(f32[1,32,128]{2,1,0:T(8,128)S(1)} %slice.458), channel_id=1, source_target_pairs={{0,8},{8,16},{16,24},{1,9},{9,17},{17,25},{2,10},{10,18},{18,26},{... | collective-permute-start | bytes 49160 | tf_op jit(solution)/shard_map/ppermute | solution.py:12
  348.0 7.8 %fusion.70 = f32[32,32,128]{2,1,0:T(8,128)} fusion(f32[32,32,128]{2,1,0:T(8,128)S(1)} %fusion.61, f32[32,32,128]{2,1,0:T(8,128)} %copy-done.18, f32[31,32,128]{2,1,0:T(8,128)S(1)} %slice.459, f32[1,32,128]{2,1,0:T(8,128)S(1)} %collective-permute-done.29, f32[32,32,128]{2,1,0:T(8,128)S(1)} %get-tuple-element.18, f32[32,31,128]{2,1,0:T(8,128)S(1)} %bitcast.68, ...), kind=kLoop, calls=%fused_computation.111 | loop fusion | flops 3670016 | bytes 5238816 | tf_op jit(solution)/shard_map/add | solution.py:98
  (198 shorter events, 129.0 us)
Async XLA Ops:
  5.1 29.7 %all-to-all-start = ((f32[4,1,128]{2,1,0:T(1,128)}), f32[4,1,128]{2,1,0:T(1,128)S(1)}, u32[]{:S(2)}, u32[]{:S(2)}) async-start(f32[4,1,128]{2,1,0:T(1,128)} %reshape.208), calls=%async_computation | async-start | bytes 4096 | tf_op jit(solution)/shard_map/all_to_all | solution.py:66
  34.8 29.3 %all-to-all-start.2 = ((f32[4,8,16,8,128]{4,3,2,1,0:T(8,128)}), f32[4,8,16,8,128]{4,3,2,1,0:T(8,128)S(1)}, u32[]{:S(2)}, u32[]{:S(2)}) async-start(f32[4,8,16,8,128]{4,3,2,1,0:T(8,128)} %bitcast.15), calls=%async_computation.2 | async-start | bytes 4194304 | tf_op jit(solution)/shard_map/all_to_all | solution.py:59
  64.1 12.8 %all-to-all-start.1 = ((f32[4,8,16]{2,0,1:T(4,128)}), f32[4,8,16]{2,0,1:T(4,128)S(1)}, u32[]{:S(2)}, u32[]{:S(2)}) async-start(f32[4,8,16]{2,0,1:T(4,128)} %copy.35), calls=%async_computation.1 | async-start | bytes 32768 | tf_op jit(solution)/shard_map/all_to_all | solution.py:65
  76.9 51.4 %all-to-all-start.3 = ((f32[4,8,16,8,128]{4,3,2,0,1:T(8,128)}), f32[4,8,16,8,128]{4,3,2,0,1:T(8,128)}, u32[]{:S(2)}, u32[]{:S(2)}) async-start(f32[4,8,16,8,128]{4,3,2,0,1:T(8,128)} %copy.37), calls=%async_computation.3 | async-start | bytes 4194304 | tf_op jit(solution)/shard_map/all_to_all | solution.py:58
  81.3 8.3 %collective-permute-start = (f32[1,32,128]{2,1,0:T(8,128)S(1)}, f32[1,32,128]{2,1,0:T(8,128)S(1)}, u32[]{:S(2)}, u32[]{:S(2)}) collective-permute-start(f32[1,32,128]{2,1,0:T(8,128)S(1)} %slice.297), channel_id=1, source_target_pairs={{8,0},{16,8},{24,16},{9,1},{17,9},{25,17},{10,2},{18,10},{26,18},{... | collective-permute-start | bytes 49160 | tf_op jit(solution)/shard_map/ppermute | solution.py:12
  82.7 10.1 %collective-permute-start.2 = (f32[32,1,128]{2,1,0:T(1,128)S(1)}, f32[32,1,128]{2,1,0:T(1,128)S(1)}, u32[]{:S(2)}, u32[]{:S(2)}) collective-permute-start(f32[32,1,128]{2,1,0:T(1,128)S(1)} %slice.301), channel_id=1, source_target_pairs={{1,0},{2,1},{3,2},{4,3},{5,4},{6,5},{7,6},{9,8},{10,9},{11,10},{12... | collective-permute-start | bytes 49160 | tf_op jit(solution)/shard_map/ppermute | solution.py:12
  98.0 37.5 %collective-permute-start.1 = (f32[1,32,128]{2,1,0:T(8,128)S(1)}, f32[1,32,128]{2,1,0:T(8,128)S(1)}, u32[]{:S(2)}, u32[]{:S(2)}) collective-permute-start(f32[1,32,128]{2,1,0:T(8,128)S(1)} %slice.384), channel_id=1, source_target_pairs={{0,8},{8,16},{16,24},{1,9},{9,17},{17,25},{2,10},{10,18},{18,26},{... | collective-permute-start | bytes 49160 | tf_op jit(solution)/shard_map/ppermute | solution.py:12
  99.4 36.2 %collective-permute-start.3 = (f32[32,1,128]{2,1,0:T(1,128)S(1)}, f32[32,1,128]{2,1,0:T(1,128)S(1)}, u32[]{:S(2)}, u32[]{:S(2)}) collective-permute-start(f32[32,1,128]{2,1,0:T(1,128)S(1)} %slice.386), channel_id=1, source_target_pairs={{0,1},{1,2},{2,3},{3,4},{4,5},{5,6},{6,7},{8,9},{9,10},{10,11},{11... | collective-permute-start | bytes 49160 | tf_op jit(solution)/shard_map/ppermute | solution.py:12
  143.9 5.6 %collective-permute-start.6 = (f32[32,1,128]{2,1,0:T(1,128)S(1)}, f32[32,1,128]{2,1,0:T(1,128)S(1)}, u32[]{:S(2)}, u32[]{:S(2)}) collective-permute-start(f32[32,1,128]{2,1,0:T(1,128)S(1)} %slice.395), channel_id=1, source_target_pairs={{1,0},{2,1},{3,2},{4,3},{5,4},{6,5},{7,6},{9,8},{10,9},{11,10},{12... | collective-permute-start | bytes 49160 | tf_op jit(solution)/shard_map/ppermute | solution.py:12
  154.3 18.8 %collective-permute-start.5 = (f32[1,32,128]{2,1,0:T(8,128)S(1)}, f32[1,32,128]{2,1,0:T(8,128)S(1)}, u32[]{:S(2)}, u32[]{:S(2)}) collective-permute-start(f32[1,32,128]{2,1,0:T(8,128)S(1)} %slice.392), channel_id=1, source_target_pairs={{0,8},{8,16},{16,24},{1,9},{9,17},{17,25},{2,10},{10,18},{18,26},{... | collective-permute-start | bytes 49160 | tf_op jit(solution)/shard_map/ppermute | solution.py:12
  156.4 16.8 %collective-permute-start.7 = (f32[32,1,128]{2,1,0:T(1,128)S(1)}, f32[32,1,128]{2,1,0:T(1,128)S(1)}, u32[]{:S(2)}, u32[]{:S(2)}) collective-permute-start(f32[32,1,128]{2,1,0:T(1,128)S(1)} %slice.396), channel_id=1, source_target_pairs={{0,1},{1,2},{2,3},{3,4},{4,5},{5,6},{6,7},{8,9},{9,10},{10,11},{11... | collective-permute-start | bytes 49160 | tf_op jit(solution)/shard_map/ppermute | solution.py:12
  180.3 5.8 %collective-permute-start.10 = (f32[32,1,128]{2,1,0:T(1,128)S(1)}, f32[32,1,128]{2,1,0:T(1,128)S(1)}, u32[]{:S(2)}, u32[]{:S(2)}) collective-permute-start(f32[32,1,128]{2,1,0:T(1,128)S(1)} %slice.406), channel_id=1, source_target_pairs={{1,0},{2,1},{3,2},{4,3},{5,4},{6,5},{7,6},{9,8},{10,9},{11,10},{12... | collective-permute-start | bytes 49160 | tf_op jit(solution)/shard_map/ppermute | solution.py:12
  189.8 12.5 %collective-permute-start.11 = (f32[32,1,128]{2,1,0:T(1,128)S(1)}, f32[32,1,128]{2,1,0:T(1,128)S(1)}, u32[]{:S(2)}, u32[]{:S(2)}) collective-permute-start(f32[32,1,128]{2,1,0:T(1,128)S(1)} %slice.407), channel_id=1, source_target_pairs={{0,1},{1,2},{2,3},{3,4},{4,5},{5,6},{6,7},{8,9},{9,10},{10,11},{11... | collective-permute-start | bytes 49160 | tf_op jit(solution)/shard_map/ppermute | solution.py:12
  194.4 8.0 %collective-permute-start.9 = (f32[1,32,128]{2,1,0:T(8,128)S(1)}, f32[1,32,128]{2,1,0:T(8,128)S(1)}, u32[]{:S(2)}, u32[]{:S(2)}) collective-permute-start(f32[1,32,128]{2,1,0:T(8,128)S(1)} %slice.403), channel_id=1, source_target_pairs={{0,8},{8,16},{16,24},{1,9},{9,17},{17,25},{2,10},{10,18},{18,26},{... | collective-permute-start | bytes 49160 | tf_op jit(solution)/shard_map/ppermute | solution.py:12
  210.6 6.3 %collective-permute-start.14 = (f32[32,1,128]{2,1,0:T(1,128)S(1)}, f32[32,1,128]{2,1,0:T(1,128)S(1)}, u32[]{:S(2)}, u32[]{:S(2)}) collective-permute-start(f32[32,1,128]{2,1,0:T(1,128)S(1)} %slice.417), channel_id=1, source_target_pairs={{1,0},{2,1},{3,2},{4,3},{5,4},{6,5},{7,6},{9,8},{10,9},{11,10},{12... | collective-permute-start | bytes 49160 | tf_op jit(solution)/shard_map/ppermute | solution.py:12
  221.6 10.7 %collective-permute-start.13 = (f32[1,32,128]{2,1,0:T(8,128)S(1)}, f32[1,32,128]{2,1,0:T(8,128)S(1)}, u32[]{:S(2)}, u32[]{:S(2)}) collective-permute-start(f32[1,32,128]{2,1,0:T(8,128)S(1)} %slice.414), channel_id=1, source_target_pairs={{0,8},{8,16},{16,24},{1,9},{9,17},{17,25},{2,10},{10,18},{18,26},{... | collective-permute-start | bytes 49160 | tf_op jit(solution)/shard_map/ppermute | solution.py:12
  223.7 8.6 %collective-permute-start.15 = (f32[32,1,128]{2,1,0:T(1,128)S(1)}, f32[32,1,128]{2,1,0:T(1,128)S(1)}, u32[]{:S(2)}, u32[]{:S(2)}) collective-permute-start(f32[32,1,128]{2,1,0:T(1,128)S(1)} %slice.418), channel_id=1, source_target_pairs={{0,1},{1,2},{2,3},{3,4},{4,5},{5,6},{6,7},{8,9},{9,10},{10,11},{11... | collective-permute-start | bytes 49160 | tf_op jit(solution)/shard_map/ppermute | solution.py:12
  240.9 5.6 %collective-permute-start.18 = (f32[32,1,128]{2,1,0:T(1,128)S(1)}, f32[32,1,128]{2,1,0:T(1,128)S(1)}, u32[]{:S(2)}, u32[]{:S(2)}) collective-permute-start(f32[32,1,128]{2,1,0:T(1,128)S(1)} %slice.428), channel_id=1, source_target_pairs={{1,0},{2,1},{3,2},{4,3},{5,4},{6,5},{7,6},{9,8},{10,9},{11,10},{12... | collective-permute-start | bytes 49160 | tf_op jit(solution)/shard_map/ppermute | solution.py:12
  250.5 10.9 %collective-permute-start.17 = (f32[1,32,128]{2,1,0:T(8,128)S(1)}, f32[1,32,128]{2,1,0:T(8,128)S(1)}, u32[]{:S(2)}, u32[]{:S(2)}) collective-permute-start(f32[1,32,128]{2,1,0:T(8,128)S(1)} %slice.425), channel_id=1, source_target_pairs={{0,8},{8,16},{16,24},{1,9},{9,17},{17,25},{2,10},{10,18},{18,26},{... | collective-permute-start | bytes 49160 | tf_op jit(solution)/shard_map/ppermute | solution.py:12
  254.1 7.2 %collective-permute-start.19 = (f32[32,1,128]{2,1,0:T(1,128)S(1)}, f32[32,1,128]{2,1,0:T(1,128)S(1)}, u32[]{:S(2)}, u32[]{:S(2)}) collective-permute-start(f32[32,1,128]{2,1,0:T(1,128)S(1)} %slice.429), channel_id=1, source_target_pairs={{0,1},{1,2},{2,3},{3,4},{4,5},{5,6},{6,7},{8,9},{9,10},{10,11},{11... | collective-permute-start | bytes 49160 | tf_op jit(solution)/shard_map/ppermute | solution.py:12
  268.1 5.3 %collective-permute-start.20 = (f32[1,32,128]{2,1,0:T(8,128)S(1)}, f32[1,32,128]{2,1,0:T(8,128)S(1)}, u32[]{:S(2)}, u32[]{:S(2)}) collective-permute-start(f32[1,32,128]{2,1,0:T(8,128)S(1)} %slice.435), channel_id=1, source_target_pairs={{8,0},{16,8},{24,16},{9,1},{17,9},{25,17},{10,2},{18,10},{26,18},{... | collective-permute-start | bytes 49160 | tf_op jit(solution)/shard_map/ppermute | solution.py:12
  269.5 5.6 %collective-permute-start.22 = (f32[32,1,128]{2,1,0:T(1,128)S(1)}, f32[32,1,128]{2,1,0:T(1,128)S(1)}, u32[]{:S(2)}, u32[]{:S(2)}) collective-permute-start(f32[32,1,128]{2,1,0:T(1,128)S(1)} %slice.439), channel_id=1, source_target_pairs={{1,0},{2,1},{3,2},{4,3},{5,4},{6,5},{7,6},{9,8},{10,9},{11,10},{12... | collective-permute-start | bytes 49160 | tf_op jit(solution)/shard_map/ppermute | solution.py:12
  279.1 11.0 %collective-permute-start.21 = (f32[1,32,128]{2,1,0:T(8,128)S(1)}, f32[1,32,128]{2,1,0:T(8,128)S(1)}, u32[]{:S(2)}, u32[]{:S(2)}) collective-permute-start(f32[1,32,128]{2,1,0:T(8,128)S(1)} %slice.436), channel_id=1, source_target_pairs={{0,8},{8,16},{16,24},{1,9},{9,17},{17,25},{2,10},{10,18},{18,26},{... | collective-permute-start | bytes 49160 | tf_op jit(solution)/shard_map/ppermute | solution.py:12
  283.1 7.0 %collective-permute-start.23 = (f32[32,1,128]{2,1,0:T(1,128)S(1)}, f32[32,1,128]{2,1,0:T(1,128)S(1)}, u32[]{:S(2)}, u32[]{:S(2)}) collective-permute-start(f32[32,1,128]{2,1,0:T(1,128)S(1)} %slice.440), channel_id=1, source_target_pairs={{0,1},{1,2},{2,3},{3,4},{4,5},{5,6},{6,7},{8,9},{9,10},{10,11},{11... | collective-permute-start | bytes 49160 | tf_op jit(solution)/shard_map/ppermute | solution.py:12
  296.9 5.3 %collective-permute-start.24 = (f32[1,32,128]{2,1,0:T(8,128)S(1)}, f32[1,32,128]{2,1,0:T(8,128)S(1)}, u32[]{:S(2)}, u32[]{:S(2)}) collective-permute-start(f32[1,32,128]{2,1,0:T(8,128)S(1)} %slice.446), channel_id=1, source_target_pairs={{8,0},{16,8},{24,16},{9,1},{17,9},{25,17},{10,2},{18,10},{26,18},{... | collective-permute-start | bytes 49160 | tf_op jit(solution)/shard_map/ppermute | solution.py:12
  298.3 5.6 %collective-permute-start.26 = (f32[32,1,128]{2,1,0:T(1,128)S(1)}, f32[32,1,128]{2,1,0:T(1,128)S(1)}, u32[]{:S(2)}, u32[]{:S(2)}) collective-permute-start(f32[32,1,128]{2,1,0:T(1,128)S(1)} %slice.450), channel_id=1, source_target_pairs={{1,0},{2,1},{3,2},{4,3},{5,4},{6,5},{7,6},{9,8},{10,9},{11,10},{12... | collective-permute-start | bytes 49160 | tf_op jit(solution)/shard_map/ppermute | solution.py:12
  307.9 11.0 %collective-permute-start.25 = (f32[1,32,128]{2,1,0:T(8,128)S(1)}, f32[1,32,128]{2,1,0:T(8,128)S(1)}, u32[]{:S(2)}, u32[]{:S(2)}) collective-permute-start(f32[1,32,128]{2,1,0:T(8,128)S(1)} %slice.447), channel_id=1, source_target_pairs={{0,8},{8,16},{16,24},{1,9},{9,17},{17,25},{2,10},{10,18},{18,26},{... | collective-permute-start | bytes 49160 | tf_op jit(solution)/shard_map/ppermute | solution.py:12
  311.9 7.0 %collective-permute-start.27 = (f32[32,1,128]{2,1,0:T(1,128)S(1)}, f32[32,1,128]{2,1,0:T(1,128)S(1)}, u32[]{:S(2)}, u32[]{:S(2)}) collective-permute-start(f32[32,1,128]{2,1,0:T(1,128)S(1)} %slice.451), channel_id=1, source_target_pairs={{0,1},{1,2},{2,3},{3,4},{4,5},{5,6},{6,7},{8,9},{9,10},{10,11},{11... | collective-permute-start | bytes 49160 | tf_op jit(solution)/shard_map/ppermute | solution.py:12
  325.6 5.3 %collective-permute-start.28 = (f32[1,32,128]{2,1,0:T(8,128)S(1)}, f32[1,32,128]{2,1,0:T(8,128)S(1)}, u32[]{:S(2)}, u32[]{:S(2)}) collective-permute-start(f32[1,32,128]{2,1,0:T(8,128)S(1)} %slice.457), channel_id=1, source_target_pairs={{8,0},{16,8},{24,16},{9,1},{17,9},{25,17},{10,2},{18,10},{26,18},{... | collective-permute-start | bytes 49160 | tf_op jit(solution)/shard_map/ppermute | solution.py:12
  327.1 5.6 %collective-permute-start.30 = (f32[32,1,128]{2,1,0:T(1,128)S(1)}, f32[32,1,128]{2,1,0:T(1,128)S(1)}, u32[]{:S(2)}, u32[]{:S(2)}) collective-permute-start(f32[32,1,128]{2,1,0:T(1,128)S(1)} %slice.461), channel_id=1, source_target_pairs={{1,0},{2,1},{3,2},{4,3},{5,4},{6,5},{7,6},{9,8},{10,9},{11,10},{12... | collective-permute-start | bytes 49160 | tf_op jit(solution)/shard_map/ppermute | solution.py:12
  337.4 10.6 %collective-permute-start.29 = (f32[1,32,128]{2,1,0:T(8,128)S(1)}, f32[1,32,128]{2,1,0:T(8,128)S(1)}, u32[]{:S(2)}, u32[]{:S(2)}) collective-permute-start(f32[1,32,128]{2,1,0:T(8,128)S(1)} %slice.458), channel_id=1, source_target_pairs={{0,8},{8,16},{16,24},{1,9},{9,17},{17,25},{2,10},{10,18},{18,26},{... | collective-permute-start | bytes 49160 | tf_op jit(solution)/shard_map/ppermute | solution.py:12
  341.4 6.6 %collective-permute-start.31 = (f32[32,1,128]{2,1,0:T(1,128)S(1)}, f32[32,1,128]{2,1,0:T(1,128)S(1)}, u32[]{:S(2)}, u32[]{:S(2)}) collective-permute-start(f32[32,1,128]{2,1,0:T(1,128)S(1)} %slice.462), channel_id=1, source_target_pairs={{0,1},{1,2},{2,3},{3,4},{4,5},{5,6},{6,7},{8,9},{9,10},{10,11},{11... | collective-permute-start | bytes 49160 | tf_op jit(solution)/shard_map/ppermute | solution.py:12
  (29 other events, 192.7 us)
where the time goes:
time: 362 us; the launch traced here: 356 us
  starting transfers between devices  115 us (32%)
  other arithmetic  113 us (31%)
  waiting for transfers between devices  74.2 us (20%)
  local copies, waits for them, and re-layouts  52.6 us (15%)
    ppermute x32, starting transfers between devices, shifted(): return lax.ppermute(block, axis, route)  96.2 us
    add x8, other arithmetic, per_device(): pressure - courant * stiffness * divergence + courant * stiffness * source  55.7 us
    ppermute x32, waiting for transfers between devices, shifted(): return lax.ppermute(block, axis, route)  31.4 us
    sub x8, other arithmetic, per_device(): vel_z = vel_z - courant * buoyancy * (next_z - pressure)  27.3 us
    scatter x1, local copies, waits for them, and re-layouts, per_device(): jnp.zeros((devices * slots, steps, layers), jnp.float32).at[position]  24 us
    all_to_all x1, waiting for transfers between devices, per_device(): lax.all_to_all(outgoing, 'gx', split_axis=0, concat_axis=0, tiled=True)  23.8 us
    scatter-add x8, other arithmetic, per_device(): source = jnp.zeros((tile_cells, layers), jnp.float32).at[holder['cells']]...  22.4 us
    all_to_all x1, waiting for transfers between devices, per_device(): lax.all_to_all(lax.all_to_all(outgoing, 'gx', split_axis=0, concat_axis=0...  13.9 us
  transfers between devices with their start and end apart: 36, of which 18 were waited for; matrix products, arithmetic and copies ran while one was open for 21% of the time, Pallas kernels for 0%

commit v1 on v0

v1 whole, which is shorter than its diff:
```python
import functools

import jax
import jax.numpy as jnp
from jax import lax
from jax.experimental import pallas as pl
from jax.experimental.pallas import tpu as pltpu
from jax.sharding import PartitionSpec as P

courant = 0.55
MESH = pl.DeviceIdType.MESH
LANES = 128


def pack_kernel(plan, tile_ref, cell_ref, panel_ref, out_ref, head_ref, count_ref):
    size_x, size_y, slots, per_chunk, rows, group = plan
    devices = size_x * size_y
    columns, steps, layers = panel_ref.shape
    width = cell_ref.shape[1]
    me = lax.axis_index("gx") * size_y + lax.axis_index("gy")
    base = lax.rem(me, group) * rows
    lane = lax.broadcasted_iota(jnp.int32, (1, LANES), 1)

    @pl.loop(0, devices)
    def _(d):
        count_ref[d] = 0
        head_ref[d] = jnp.zeros((1, LANES), jnp.float32)
        for c in range(steps // per_chunk):
            out_ref[c, d] = jnp.zeros((rows, layers), jnp.float32)

    @pl.loop(0, columns)
    def _(c):
        t = tile_ref[c]
        slot = count_ref[t]
        count_ref[t] = slot + 1
        cell = cell_ref[c // width, lax.rem(c, width)]
        number = (cell + 1).astype(jnp.float32)
        spot = lane - (base + slot)
        row = head_ref[t]
        for j in range(per_chunk):
            row = jnp.where(spot == j * slots, number, row)
        head_ref[t] = row
        for s in range(steps):
            out_ref[s // per_chunk, t, pl.ds((s % per_chunk) * slots + slot, 1), :] = panel_ref[c, pl.ds(s, 1), :]


def wave_kernel(
    plan,
    p_in,
    vx_in,
    vy_in,
    vz_in,
    mat_in,
    dens,
    speed,
    send,
    head,
    P_,
    VX,
    VY,
    VZ,
    CB,
    CS,
    recv,
    head_recv,
    onehot,
    rhs,
    source,
    hx_lo,
    hx_hi,
    hy_lo,
    hy_hi,
    x_out,
    y_out,
    vxh,
    cbxh,
    vyh,
    cbyh,
    y_start,
    bulk_send,
    bulk_recv,
    head_sem,
    halo_send,
    halo_recv,
    start_send,
    start_recv,
):
    size_x, size_y, slots, per_chunk, rows, group = plan
    devices = size_x * size_y
    cx, cy, nz = p_in.shape
    chunks = recv.shape[0]
    steps = chunks * per_chunk
    gx, gy = lax.axis_index("gx"), lax.axis_index("gy")
    me = gx * size_y + gy
    has_xl, has_xu = gx > 0, gx < size_x - 1
    has_yl, has_yu = gy > 0, gy < size_y - 1
    x_up, x_down = (gx + 1, gy), (gx - 1, gy)
    y_up, y_down = (gx, gy + 1), (gx, gy - 1)

    barrier = pltpu.get_barrier_semaphore()

    @pl.loop(1, devices)
    def _(k):
        t = lax.rem(me + k, devices)
        pl.semaphore_signal(barrier, inc=1, device_id=(t // size_y, lax.rem(t, size_y)), device_id_type=MESH)

    b_of, k_of = [], []
    for m in range(dens.shape[0]):
        d = jnp.full((1, nz), dens[m], jnp.float32)
        c = jnp.full((1, nz), speed[m], jnp.float32)
        b_of.append(courant * (1.0 / d))
        k_of.append(courant * (d * c * c))

    @pl.loop(0, cx)
    def _(i):
        mat = mat_in[i]
        b = jnp.zeros((cy, nz), jnp.float32)
        k = jnp.zeros((cy, nz), jnp.float32)
        for m in range(dens.shape[0]):
            b = jnp.where(mat == m, b_of[m], b)
            k = jnp.where(mat == m, k_of[m], k)
        CB[i] = b
        CS[i] = k
        p = p_in[i]
        vy = vy_in[i]
        P_[i] = p
        VX[i] = vx_in[i]
        VY[i] = vy
        VZ[i] = vz_in[i]
        y_out[0, 0, pl.ds(i, 1), :] = p[0:1]
        y_out[0, 1, pl.ds(i, 1), :] = p[cy - 1 : cy]
        y_start[0, pl.ds(i, 1), :] = vy[cy - 1 : cy]
        y_start[1, pl.ds(i, 1), :] = b[cy - 1 : cy]

    x_out[0, 0] = p_in[0]
    x_out[0, 1] = p_in[cx - 1]

    @pl.when(jnp.logical_not(has_xl))
    def _():
        vxh[...] = jnp.zeros_like(vxh)
        cbxh[...] = jnp.zeros_like(cbxh)
        hx_lo[...] = jnp.zeros_like(hx_lo)

    @pl.when(jnp.logical_not(has_xu))
    def _():
        hx_hi[...] = jnp.zeros_like(hx_hi)

    @pl.when(jnp.logical_not(has_yl))
    def _():
        vyh[...] = jnp.zeros_like(vyh)
        cbyh[...] = jnp.zeros_like(cbyh)
        hy_lo[...] = jnp.zeros_like(hy_lo)

    @pl.when(jnp.logical_not(has_yu))
    def _():
        hy_hi[...] = jnp.zeros_like(hy_hi)

    pl.semaphore_wait(barrier, devices - 1)

    def remote(src, dst, send_sem, recv_sem, device):
        return pltpu.make_async_remote_copy(
            src_ref=src, dst_ref=dst, send_sem=send_sem, recv_sem=recv_sem, device_id=device, device_id_type=MESH
        )

    def halo(s, direction):
        src, dst, device = (
            (x_out.at[s, 0], hx_hi.at[s], x_down),
            (x_out.at[s, 1], hx_lo.at[s], x_up),
            (y_out.at[s, 0], hy_hi.at[s], y_down),
            (y_out.at[s, 1], hy_lo.at[s], y_up),
        )[direction]
        return remote(src, dst, halo_send.at[s, direction], halo_recv.at[s, direction], device)

    senders = (has_xl, has_xu, has_yl, has_yu)
    receivers = (has_xu, has_xl, has_yu, has_yl)

    def halo_start(s):
        for direction in range(4):

            @pl.when(senders[direction])
            def _():
                halo(s, direction).start()

    def halo_wait(s):
        for direction in range(4):

            @pl.when(receivers[direction])
            def _():
                halo(s, direction).wait_recv()

    def first(which):
        src, dst, device = (
            (vx_in.at[cx - 1], vxh, x_up),
            (CB.at[cx - 1], cbxh, x_up),
            (y_start.at[0], vyh, y_up),
            (y_start.at[1], cbyh, y_up),
        )[which]
        return remote(src, dst, start_send.at[which], start_recv.at[which], device)

    def bulk_start(c):
        pltpu.make_async_copy(send.at[c, me], recv.at[c, me], bulk_recv.at[c]).start()

        @pl.loop(1, devices)
        def _(k):
            t = lax.rem(me + k, devices)
            remote(
                send.at[c, t], recv.at[c, me], bulk_send.at[c], bulk_recv.at[c], (t // size_y, lax.rem(t, size_y))
            ).start()

    halo_start(0)
    for which in range(4):

        @pl.when((has_xu, has_xu, has_yu, has_yu)[which])
        def _():
            first(which).start()

    pltpu.make_async_copy(head.at[me], head_recv.at[me], head_sem.at[1]).start()

    @pl.loop(1, devices)
    def _(k):
        t = lax.rem(me + k, devices)
        remote(
            head.at[t], head_recv.at[me], head_sem.at[0], head_sem.at[1], (t // size_y, lax.rem(t, size_y))
        ).start()

    bulk_start(0)
    if chunks > 1:
        bulk_start(1)

    for which in range(4):

        @pl.when((has_xl, has_xl, has_yl, has_yl)[which])
        def _():
            first(which).wait_recv()

    pltpu.make_async_copy(head_recv, head_recv, head_sem.at[1]).wait()
    block = min(128, cx * cy)
    for r in range(devices // group):
        cells = jnp.sum(head_recv[pl.ds(r * group, group)], axis=0)

        @pl.loop(0, cx * cy // block)
        def _(m):
            number = lax.broadcasted_iota(jnp.int32, (block, LANES), 0) + (m * block + 1)
            onehot[pl.ds(pl.multiple_of(m * block, block), block), r * LANES : (r + 1) * LANES] = jnp.where(
                number.astype(jnp.float32) == cells, 1.0, 0.0
            ).astype(jnp.bfloat16)

    row = lax.broadcasted_iota(jnp.int32, (cy, nz), 0)
    lane = lax.broadcasted_iota(jnp.int32, (cy, nz), 1)

    @pl.loop(0, steps)
    def _(s):
        c = s // per_chunk

        @pl.when(lax.rem(s, per_chunk) == 0)
        def _():
            pltpu.make_async_copy(recv.at[c], recv.at[c], bulk_recv.at[c]).wait()

        @pl.loop(0, devices)
        def _(d):
            values = recv[c, d]
            if per_chunk > 1:
                step_of = lax.broadcasted_iota(jnp.int32, (rows, nz), 0) // slots
                values = jnp.where(step_of == lax.rem(s, per_chunk), values, 0.0)
            high = values.astype(jnp.bfloat16)
            low = (values - high.astype(jnp.float32)).astype(jnp.bfloat16)
            at = pl.ds(pl.multiple_of(d * rows, rows), rows)
            rhs[at, 0:nz] = high
            rhs[at, nz : 2 * nz] = low

        mm = min(256, cx * cy)

        @pl.loop(0, cx * cy // mm)
        def _(m):
            at = pl.ds(pl.multiple_of(m * mm, mm), mm)
            out = jnp.dot(onehot[at, :], rhs[...], preferred_element_type=jnp.float32)
            source[at, :] = out[:, :nz] + out[:, nz:]

        halo_wait(s)

        def plane(i, p, p_next, vx_prev):
            b = CB[i]
            at = pl.ds(i, 1)
            vx = VX[i] - b * (p_next - p)
            p_yn = jnp.where(row == cy - 1, hy_hi[s, at, :], pltpu.roll(p, cy - 1, 0))
            vy = VY[i] - b * (p_yn - p)
            p_zn = jnp.where(lane == nz - 1, 0.0, pltpu.roll(p, nz - 1, 1))
            vz = VZ[i] - b * (p_zn - p)
            edge = vyh[at, :] - cbyh[at, :] * (p[0:1] - hy_lo[s, at, :])
            vyh[at, :] = edge
            vy_prev = jnp.where(row == 0, edge, pltpu.roll(vy, 1, 0))
            vz_prev = jnp.where(lane == 0, 0.0, pltpu.roll(vz, 1, 1))
            divergence = (vx - vx_prev) + (vy - vy_prev)
            divergence = divergence + (vz - vz_prev)
            src = source[pl.ds(pl.multiple_of(i * cy, cy), cy), :]
            new = p + CS[i] * (src - divergence)
            VX[i] = vx
            VY[i] = vy
            VZ[i] = vz
            P_[i] = new

            @pl.when(s < steps - 1)
            def _():
                y_out[s + 1, 0, at, :] = new[0:1]
                y_out[s + 1, 1, at, :] = new[cy - 1 : cy]

            return new, vx

        p0 = P_[0]
        edge_x = vxh[...] - cbxh[...] * (p0 - hx_lo[s])
        vxh[...] = edge_x

        def body(i, carry):
            p, vx_prev = carry
            p_next = P_[i + 1]
            _, vx = plane(i, p, p_next, vx_prev)
            return p_next, vx

        p_last, vx_last = lax.fori_loop(0, cx - 1, body, (p0, edge_x))
        new_last, _ = plane(cx - 1, p_last, hx_hi[s], vx_last)

        @pl.when(s < steps - 1)
        def _():
            x_out[s + 1, 0] = P_[0]
            x_out[s + 1, 1] = new_last
            halo_start(s + 1)

        @pl.when(jnp.logical_and(lax.rem(s, per_chunk) == per_chunk - 1, c + 2 < chunks))
        def _():
            bulk_start(c + 2)

    others = devices - 1
    pltpu.make_async_copy(head.at[pl.ds(0, others)], head.at[pl.ds(0, others)], head_sem.at[0]).wait()

    @pl.loop(0, chunks)
    def _(c):
        whole = send.at[c, pl.ds(0, others)]
        pltpu.make_async_copy(whole, whole, bulk_send.at[c]).wait()

    @pl.loop(0, steps)
    def _(s):
        for direction in range(4):

            @pl.when(senders[direction])
            def _():
                halo(s, direction).wait_send()

    for which in range(4):

        @pl.when((has_xu, has_xu, has_yu, has_yu)[which])
        def _():
            first(which).wait_send()


def per_device(pressure, vel_x, vel_y, vel_z, material, density_table, speed_table, panel_vals, panel_tile, panel_cell):
    size_x = lax.axis_size("gx")
    size_y = lax.axis_size("gy")
    devices = size_x * size_y
    cx, cy, nz = pressure.shape
    steps = panel_vals.shape[2]
    columns = panel_vals.shape[0] * panel_vals.shape[1]
    slots = max(2, 2 * columns // devices)
    per_chunk = max(1, 8 // slots)
    rows = slots * per_chunk
    chunks = steps // per_chunk
    group = LANES // rows
    plan = (size_x, size_y, slots, per_chunk, rows, group)
    f32 = jnp.float32
    vmem = pl.BlockSpec(memory_space=pltpu.VMEM)
    smem = pl.BlockSpec(memory_space=pltpu.SMEM)
    send, head = pl.pallas_call(
        functools.partial(pack_kernel, plan),
        out_shape=(
            jax.ShapeDtypeStruct((chunks, devices, rows, nz), f32),
            jax.ShapeDtypeStruct((devices, 1, LANES), f32),
        ),
        in_specs=[smem, smem, vmem],
        out_specs=(vmem, vmem),
        scratch_shapes=[pltpu.SMEM((devices,), jnp.int32)],
        compiler_params=pltpu.CompilerParams(vmem_limit_bytes=16 * 1024 * 1024),
        name="pack",
    )(panel_tile.reshape(-1), panel_cell, panel_vals.reshape(columns, steps, nz))
    field = jax.ShapeDtypeStruct((cx, cy, nz), f32)
    dma = pltpu.SemaphoreType.DMA
    return pl.pallas_call(
        functools.partial(wave_kernel, plan),
        out_shape=(field,) * 4,
        in_specs=[vmem] * 5 + [smem] * 2 + [vmem] * 2,
        out_specs=(vmem,) * 4,
        scratch_shapes=[
            pltpu.VMEM((cx, cy, nz), f32),
            pltpu.VMEM((cx, cy, nz), f32),
            pltpu.VMEM((chunks, devices, rows, nz), f32),
            pltpu.VMEM((devices, 1, LANES), f32),
            pltpu.VMEM((cx * cy, devices * rows), jnp.bfloat16),
            pltpu.VMEM((devices * rows, 2 * nz), jnp.bfloat16),
            pltpu.VMEM((cx * cy, nz), f32),
            pltpu.VMEM((steps, cy, nz), f32),
            pltpu.VMEM((steps, cy, nz), f32),
            pltpu.VMEM((steps, cx, nz), f32),
            pltpu.VMEM((steps, cx, nz), f32),
            pltpu.VMEM((steps, 2, cy, nz), f32),
            pltpu.VMEM((steps, 2, cx, nz), f32),
            pltpu.VMEM((cy, nz), f32),
            pltpu.VMEM((cy, nz), f32),
            pltpu.VMEM((cx, nz), f32),
            pltpu.VMEM((cx, nz), f32),
            pltpu.VMEM((2, cx, nz), f32),
            dma((chunks,)),
            dma((chunks,)),
            dma((2,)),
            dma((steps, 4)),
            dma((steps, 4)),
            dma((4,)),
            dma((4,)),
        ],
        compiler_params=pltpu.CompilerParams(
            collective_id=0, has_side_effects=True, vmem_limit_bytes=40 * 1024 * 1024
        ),
        name="wave",
    )(pressure, vel_x, vel_y, vel_z, material, density_table, speed_table, send, head)


def solution(mesh):
    tile = P("gx", "gy", None)
    return jax.shard_map(
        per_device,
        mesh=mesh,
        in_specs=(
            tile,
            tile,
            tile,
            tile,
            tile,
            P(),
            P(),
            P(("gx", "gy"), None, None, None),
            P(("gx", "gy"), None, None),
            P(("gx", "gy"), None),
        ),
        out_specs=(tile,) * 4,
        check_vma=False,
    )
```

time: 362 us -> 102 us (0.28); the launches traced: 356 us -> 102 us
  starting transfers between devices: 115 us -> 0 us
  other arithmetic: 113 us -> 0 us
  Pallas kernels: 0 us -> 88.7 us
  waiting for transfers between devices: 74.2 us -> 0 us
  local copies, waits for them, and re-layouts: 52.6 us -> 12.3 us
    ppermute x32 -> x0, starting transfers between devices: 96.2 us -> none  [shifted(): return lax.ppermute(block, axis, route)]
    pallas_call x0 -> x2, Pallas kernels: none -> 88.7 us  [the longest x1 84 us: per_device(): pl.pallas_call(functools.partial(wave_kernel, plan), out_shape=(field,) *...]
    add x8 -> x0, other arithmetic: 55.7 us -> none  [per_device(): pressure - courant * stiffness * divergence + courant * stiffness * source]
    all_to_all x4 -> x0, waiting for transfers between devices: 42.9 us -> none  [the longest x1 23.8 us: per_device(): lax.all_to_all(outgoing, 'gx', split_axis=0, concat_axis=0, tiled=True)]
    sub x9 -> x0, other arithmetic: 31.7 us -> none  [the longest x8 27.3 us: per_device(): vel_z = vel_z - courant * buoyancy * (next_z - pressure)]
    ppermute x32 -> x0, waiting for transfers between devices: 31.4 us -> none  [shifted(): return lax.ppermute(block, axis, route)]
    scatter x2 -> x0, local copies, waits for them, and re-layouts: 25.4 us -> none  [the longest x1 24 us: per_device(): jnp.zeros((devices * slots, steps, layers), jnp.float32).at[position]]
    scatter-add x8 -> x0, other arithmetic: 22.4 us -> none  [per_device(): source = jnp.zeros((tile_cells, layers), jnp.float32).at[holder['cells']]...]
  transfers between devices with their start and end apart: 36 -> 0, of which waited for: 18 -> 0; matrix products, arithmetic and copies ran while one was open for 21% -> 0% of each run, Pallas kernels for 0% -> 0%
where the time goes in v1:
time: 102 us
  Pallas kernels  88.7 us (87%)
  local copies, waits for them, and re-layouts  12.3 us (12%)
    pallas_call x1, Pallas kernels, per_device(): pl.pallas_call(functools.partial(wave_kernel, plan), out_shape=(field,) *...  84 us
    unnamed x24, local copies, waits for them, and re-layouts  12.3 us
    pallas_call x1, Pallas kernels, per_device(): pl.pallas_call(functools.partial(pack_kernel, plan), out_shape=(jax.Shape...  4.71 us

profile of v1, /device:TPU:0, one launch (start us, length us, event | category | flops | bytes accessed | tf_op | source)
XLA Modules:
  0.0 101.6 jit_solution(4418845550351665022)
XLA Ops:
  0.6 0.0 copy-start
  0.6 1.2 %copy-done = f32[2,128,8,128]{3,2,1,0:T(8,128)S(1)} copy-done((f32[2,128,8,128]{3,2,1,0:T(8,128)S(1)}, f32[2,128,8,128]{3,2,1,0:T(8,128)}, u32[]{:S(2)}) %copy-start) | copy-done | bytes 1048600
  1.9 0.0 copy-start.6
  1.9 0.7 copy-done.6
  2.5 0.0 copy-start.7
  2.5 0.7 copy-done.7
  3.2 4.7 %pack.1 = (f32[8,32,16,128]{3,2,1,0:T(8,128)S(1)}, f32[32,1,128]{2,1,0:T(1,128)S(1)}) custom-call(s32[256]{0:T(256)S(1)} %bitcast.3, s32[2,128]{1,0:T(2,128)S(1)} %copy-done.7, f32[256,8,128]{2,1,0:T(8,128)S(1)} %bitcast.2), custom_call_target="tpu_custom_call" | custom-call | tf_op jit(solution)/shard_map/pack/pallas_call | solution.py:371
  7.9 0.0 copy-start.1
  8.0 1.0 %copy-done.1 = f32[32,32,128]{2,1,0:T(8,128)S(1)} copy-done((f32[32,32,128]{2,1,0:T(8,128)S(1)}, f32[32,32,128]{2,1,0:T(8,128)}, u32[]{:S(2)}) %copy-start.1) | copy-done | bytes 524312
  9.0 0.0 copy-start.2
  9.0 1.0 %copy-done.2 = f32[32,32,128]{2,1,0:T(8,128)S(1)} copy-done((f32[32,32,128]{2,1,0:T(8,128)S(1)}, f32[32,32,128]{2,1,0:T(8,128)}, u32[]{:S(2)}) %copy-start.2) | copy-done | bytes 524312
  10.0 0.0 copy-start.3
  10.0 1.0 %copy-done.3 = f32[32,32,128]{2,1,0:T(8,128)S(1)} copy-done((f32[32,32,128]{2,1,0:T(8,128)S(1)}, f32[32,32,128]{2,1,0:T(8,128)}, u32[]{:S(2)}) %copy-start.3) | copy-done | bytes 524312
  11.1 0.0 copy-start.4
  11.1 1.0 %copy-done.4 = f32[32,32,128]{2,1,0:T(8,128)S(1)} copy-done((f32[32,32,128]{2,1,0:T(8,128)S(1)}, f32[32,32,128]{2,1,0:T(8,128)}, u32[]{:S(2)}) %copy-start.4) | copy-done | bytes 524312
  12.1 0.0 copy-start.5
  12.1 1.0 %copy-done.5 = s32[32,32,128]{2,1,0:T(8,128)S(1)} copy-done((s32[32,32,128]{2,1,0:T(8,128)S(1)}, s32[32,32,128]{2,1,0:T(8,128)}, u32[]{:S(2)}) %copy-start.5) | copy-done | bytes 524312
  13.2 0.0 copy-start.8
  13.2 0.7 copy-done.8
  13.8 0.0 copy-start.9
  13.8 0.7 copy-done.9
  14.5 84.0 %wave.1 = (f32[32,32,128]{2,1,0:T(8,128)S(1)}, f32[32,32,128]{2,1,0:T(8,128)S(1)}, f32[32,32,128]{2,1,0:T(8,128)S(1)}, f32[32,32,128]{2,1,0:T(8,128)S(1)}) custom-call(f32[32,32,128]{2,1,0:T(8,128)S(1)} %copy-done.1, f32[32,32,128]{2,1,0:T(8,128)S(1)} %copy-done.2, f32[32,32,128]{2,1,0:T(8,128)S(1)} %copy-done.3, f32[32,32,128]{2,1,0:T(8,128)S(1)} %copy-done.4, ...), custom_call_target="tpu_custom_call" | custom-call | tf_op jit(solution)/shard_map/wave/pallas_call | solution.py:385
  98.4 0.8 copy.18
  99.2 0.8 copy.19
  100.0 0.8 copy.20
  100.8 0.8 copy.21
Async XLA Ops:
  0.6 1.2 %copy-start = (f32[2,128,8,128]{3,2,1,0:T(8,128)S(1)}, f32[2,128,8,128]{3,2,1,0:T(8,128)}, u32[]{:S(2)}) copy-start(f32[2,128,8,128]{3,2,1,0:T(8,128)} %param.17) | copy-start | bytes 3145732
  1.9 0.7 copy-start.6
  2.5 0.7 copy-start.7
  7.9 1.0 %copy-start.1 = (f32[32,32,128]{2,1,0:T(8,128)S(1)}, f32[32,32,128]{2,1,0:T(8,128)}, u32[]{:S(2)}) copy-start(f32[32,32,128]{2,1,0:T(8,128)} %p_in.1) | copy-start | bytes 1572868
  9.0 1.0 %copy-start.2 = (f32[32,32,128]{2,1,0:T(8,128)S(1)}, f32[32,32,128]{2,1,0:T(8,128)}, u32[]{:S(2)}) copy-start(f32[32,32,128]{2,1,0:T(8,128)} %vx_in.1) | copy-start | bytes 1572868
  10.0 1.0 %copy-start.3 = (f32[32,32,128]{2,1,0:T(8,128)S(1)}, f32[32,32,128]{2,1,0:T(8,128)}, u32[]{:S(2)}) copy-start(f32[32,32,128]{2,1,0:T(8,128)} %vy_in.1) | copy-start | bytes 1572868
  11.1 1.0 %copy-start.4 = (f32[32,32,128]{2,1,0:T(8,128)S(1)}, f32[32,32,128]{2,1,0:T(8,128)}, u32[]{:S(2)}) copy-start(f32[32,32,128]{2,1,0:T(8,128)} %vz_in.1) | copy-start | bytes 1572868
  12.1 1.0 %copy-start.5 = (s32[32,32,128]{2,1,0:T(8,128)S(1)}, s32[32,32,128]{2,1,0:T(8,128)}, u32[]{:S(2)}) copy-start(s32[32,32,128]{2,1,0:T(8,128)} %mat_in.1) | copy-start | bytes 1572868
  13.2 0.7 copy-start.8
  13.8 0.7 copy-start.9

commit v2 on v1

--- a/solution.py
+++ b/solution.py
@@ -59,6 +59,7 @@
     VX,
     VY,
     VZ,
+    mat,
     CB,
     CS,
     recv,
@@ -76,7 +77,9 @@
     cbxh,
     vyh,
     cbyh,
+    x_start,
     y_start,
+    load_sem,
     bulk_send,
     bulk_recv,
     head_sem,
@@ -90,6 +93,7 @@
     cx, cy, nz = p_in.shape
     chunks = recv.shape[0]
     steps = chunks * per_chunk
+    planes = 8 if cx % 8 == 0 else 1
     gx, gy = lax.axis_index("gx"), lax.axis_index("gy")
     me = gx * size_y + gy
     has_xl, has_xu = gx > 0, gx < size_x - 1
@@ -97,43 +101,19 @@
     x_up, x_down = (gx + 1, gy), (gx - 1, gy)
     y_up, y_down = (gx, gy + 1), (gx, gy - 1)
 
+    loads = [
+        pltpu.make_async_copy(src, dst, load_sem.at[n])
+        for n, (src, dst) in enumerate(((mat_in, mat), (p_in, P_), (vy_in, VY), (vx_in, VX), (vz_in, VZ)))
+    ]
+    for load in loads:
+        load.start()
+
     barrier = pltpu.get_barrier_semaphore()
 
     @pl.loop(1, devices)
     def _(k):
         t = lax.rem(me + k, devices)
         pl.semaphore_signal(barrier, inc=1, device_id=(t // size_y, lax.rem(t, size_y)), device_id_type=MESH)
-
-    b_of, k_of = [], []
-    for m in range(dens.shape[0]):
-        d = jnp.full((1, nz), dens[m], jnp.float32)
-        c = jnp.full((1, nz), speed[m], jnp.float32)
-        b_of.append(courant * (1.0 / d))
-        k_of.append(courant * (d * c * c))
-
-    @pl.loop(0, cx)
-    def _(i):
-        mat = mat_in[i]
-        b = jnp.zeros((cy, nz), jnp.float32)
-        k = jnp.zeros((cy, nz), jnp.float32)
-        for m in range(dens.shape[0]):
-            b = jnp.where(mat == m, b_of[m], b)
-            k = jnp.where(mat == m, k_of[m], k)
-        CB[i] = b
-        CS[i] = k
-        p = p_in[i]
-        vy = vy_in[i]
-        P_[i] = p
-        VX[i] = vx_in[i]
-        VY[i] = vy
-        VZ[i] = vz_in[i]
-        y_out[0, 0, pl.ds(i, 1), :] = p[0:1]
-        y_out[0, 1, pl.ds(i, 1), :] = p[cy - 1 : cy]
-        y_start[0, pl.ds(i, 1), :] = vy[cy - 1 : cy]
-        y_start[1, pl.ds(i, 1), :] = b[cy - 1 : cy]
-
-    x_out[0, 0] = p_in[0]
-    x_out[0, 1] = p_in[cx - 1]
 
     @pl.when(jnp.logical_not(has_xl))
     def _():
@@ -190,7 +170,7 @@
 
     def first(which):
         src, dst, device = (
-            (vx_in.at[cx - 1], vxh, x_up),
+            (x_start, vxh, x_up),
             (CB.at[cx - 1], cbxh, x_up),
             (y_start.at[0], vyh, y_up),
             (y_start.at[1], cbyh, y_up),
@@ -207,13 +187,6 @@
                 send.at[c, t], recv.at[c, me], bulk_send.at[c], bulk_recv.at[c], (t // size_y, lax.rem(t, size_y))
             ).start()
 
-    halo_start(0)
-    for which in range(4):
-
-        @pl.when((has_xu, has_xu, has_yu, has_yu)[which])
-        def _():
-            first(which).start()
-
     pltpu.make_async_copy(head.at[me], head_recv.at[me], head_sem.at[1]).start()
 
     @pl.loop(1, devices)
@@ -224,6 +197,46 @@
         ).start()
 
     bulk_start(0)
+    b_of, k_of = [], []
+    for m in range(dens.shape[0]):
+        d = jnp.full((1, nz), dens[m], jnp.float32)
+        c = jnp.full((1, nz), speed[m], jnp.float32)
+        b_of.append(courant * (1.0 / d))
+        k_of.append(courant * (d * c * c))
+
+    for load in loads[:3]:
+        load.wait()
+
+    @pl.loop(0, cx // planes)
+    def _(g):
+        at = pl.ds(g * planes, planes)
+        material = mat[at]
+        b = jnp.zeros(material.shape, jnp.float32)
+        k = jnp.zeros(material.shape, jnp.float32)
+        for m in range(dens.shape[0]):
+            b = jnp.where(material == m, b_of[m][None], b)
+            k = jnp.where(material == m, k_of[m][None], k)
+        CB[at] = b
+        CS[at] = k
+        p = P_[at]
+        y_out[0, 0, at] = p[:, 0:1]
+        y_out[0, 1, at] = p[:, cy - 1 : cy]
+        y_start[0, at] = VY[at][:, cy - 1 : cy]
+        y_start[1, at] = b[:, cy - 1 : cy]
+
+    x_out[0, 0] = P_[0]
+    x_out[0, 1] = P_[cx - 1]
+    for load in loads[3:]:
+        load.wait()
+    x_start[...] = VX[cx - 1]
+
+    halo_start(0)
+    for which in range(4):
+
+        @pl.when((has_xu, has_xu, has_yu, has_yu)[which])
+        def _():
+            first(which).start()
+
     if chunks > 1:
         bulk_start(1)
 
@@ -245,8 +258,8 @@
                 number.astype(jnp.float32) == cells, 1.0, 0.0
             ).astype(jnp.bfloat16)
 
-    row = lax.broadcasted_iota(jnp.int32, (cy, nz), 0)
-    lane = lax.broadcasted_iota(jnp.int32, (cy, nz), 1)
+    row = lax.broadcasted_iota(jnp.int32, (planes, cy, nz), 1)
+    lane = lax.broadcasted_iota(jnp.int32, (planes, cy, nz), 2)
 
     @pl.loop(0, steps)
     def _(s):
@@ -256,17 +269,13 @@
         def _():
             pltpu.make_async_copy(recv.at[c], recv.at[c], bulk_recv.at[c]).wait()
 
-        @pl.loop(0, devices)
-        def _(d):
-            values = recv[c, d]
-            if per_chunk > 1:
-                step_of = lax.broadcasted_iota(jnp.int32, (rows, nz), 0) // slots
-                values = jnp.where(step_of == lax.rem(s, per_chunk), values, 0.0)
-            high = values.astype(jnp.bfloat16)
-            low = (values - high.astype(jnp.float32)).astype(jnp.bfloat16)
-            at = pl.ds(pl.multiple_of(d * rows, rows), rows)
-            rhs[at, 0:nz] = high
-            rhs[at, nz : 2 * nz] = low
+        values = recv[c].reshape(devices * rows, nz)
+        if per_chunk > 1:
+            step_of = lax.rem(lax.broadcasted_iota(jnp.int32, values.shape, 0), rows) // slots
+            values = jnp.where(step_of == lax.rem(s, per_chunk), values, 0.0)
+        high = values.astype(jnp.bfloat16)
+        rhs[:, 0:nz] = high
+        rhs[:, nz : 2 * nz] = (values - high.astype(jnp.float32)).astype(jnp.bfloat16)
 
         mm = min(256, cx * cy)
 
@@ -278,51 +287,46 @@
 
         halo_wait(s)
 
-        def plane(i, p, p_next, vx_prev):
-            b = CB[i]
-            at = pl.ds(i, 1)
-            vx = VX[i] - b * (p_next - p)
-            p_yn = jnp.where(row == cy - 1, hy_hi[s, at, :], pltpu.roll(p, cy - 1, 0))
-            vy = VY[i] - b * (p_yn - p)
-            p_zn = jnp.where(lane == nz - 1, 0.0, pltpu.roll(p, nz - 1, 1))
-            vz = VZ[i] - b * (p_zn - p)
-            edge = vyh[at, :] - cbyh[at, :] * (p[0:1] - hy_lo[s, at, :])
-            vyh[at, :] = edge
-            vy_prev = jnp.where(row == 0, edge, pltpu.roll(vy, 1, 0))
-            vz_prev = jnp.where(lane == 0, 0.0, pltpu.roll(vz, 1, 1))
+        def block_of(i, after, vx_before):
+            at = pl.ds(i, planes)
+            b = CB[at]
+            p = P_[at]
+            p_xn = jnp.concatenate([p[1:], after[None]], axis=0)
+            vx = VX[at] - b * (p_xn - p)
+            p_yn = jnp.where(row == cy - 1, hy_hi[s, at], pltpu.roll(p, cy - 1, 1))
+            vy = VY[at] - b * (p_yn - p)
+            p_zn = jnp.where(lane == nz - 1, 0.0, pltpu.roll(p, nz - 1, 2))
+            vz = VZ[at] - b * (p_zn - p)
+            edge = vyh[at] - cbyh[at] * (p[:, 0:1] - hy_lo[s, at])
+            vx_prev = jnp.concatenate([vx_before[None], vx[:-1]], axis=0)
+            vy_prev = jnp.where(row == 0, edge, pltpu.roll(vy, 1, 1))
+            vz_prev = jnp.where(lane == 0, 0.0, pltpu.roll(vz, 1, 2))
             divergence = (vx - vx_prev) + (vy - vy_prev)
             divergence = divergence + (vz - vz_prev)
-            src = source[pl.ds(pl.multiple_of(i * cy, cy), cy), :]
-            new = p + CS[i] * (src - divergence)
-            VX[i] = vx
-            VY[i] = vy
-            VZ[i] = vz
-            P_[i] = new
-
-            @pl.when(s < steps - 1)
-            def _():
-                y_out[s + 1, 0, at, :] = new[0:1]
-                y_out[s + 1, 1, at, :] = new[cy - 1 : cy]
-
-            return new, vx
-
-        p0 = P_[0]
-        edge_x = vxh[...] - cbxh[...] * (p0 - hx_lo[s])
+            src = source[pl.ds(pl.multiple_of(i * cy, cy), planes * cy), :].reshape(planes, cy, nz)
+            new = p + CS[at] * (src - divergence)
+            vyh[at] = edge
+            VX[at] = vx
+            VY[at] = vy
+            VZ[at] = vz
+            P_[at] = new
+            y_out[s + 1, 0, at] = new[:, 0:1]
+            y_out[s + 1, 1, at] = new[:, cy - 1 : cy]
+            return vx[planes - 1]
+
+        edge_x = vxh[...] - cbxh[...] * (P_[0] - hx_lo[s])
         vxh[...] = edge_x
 
-        def body(i, carry):
-            p, vx_prev = carry
-            p_next = P_[i + 1]
-            _, vx = plane(i, p, p_next, vx_prev)
-            return p_next, vx
-
-        p_last, vx_last = lax.fori_loop(0, cx - 1, body, (p0, edge_x))
-        new_last, _ = plane(cx - 1, p_last, hx_hi[s], vx_last)
+        def body(g, vx_before):
+            return block_of(g * planes, P_[(g + 1) * planes], vx_before)
+
+        vx_last = lax.fori_loop(0, cx // planes - 1, body, edge_x)
+        block_of(cx - planes, hx_hi[s], vx_last)
 
         @pl.when(s < steps - 1)
         def _():
             x_out[s + 1, 0] = P_[0]
-            x_out[s + 1, 1] = new_last
+            x_out[s + 1, 1] = P_[cx - 1]
             halo_start(s + 1)
 
         @pl.when(jnp.logical_and(lax.rem(s, per_chunk) == per_chunk - 1, c + 2 < chunks))
@@ -368,6 +372,7 @@
     f32 = jnp.float32
     vmem = pl.BlockSpec(memory_space=pltpu.VMEM)
     smem = pl.BlockSpec(memory_space=pltpu.SMEM)
+    hbm = pl.BlockSpec(memory_space=pltpu.HBM)
     send, head = pl.pallas_call(
         functools.partial(pack_kernel, plan),
         out_shape=(
@@ -385,9 +390,10 @@
     return pl.pallas_call(
         functools.partial(wave_kernel, plan),
         out_shape=(field,) * 4,
-        in_specs=[vmem] * 5 + [smem] * 2 + [vmem] * 2,
+        in_specs=[hbm] * 5 + [smem] * 2 + [vmem] * 2,
         out_specs=(vmem,) * 4,
         scratch_shapes=[
+            pltpu.VMEM((cx, cy, nz), jnp.int32),
             pltpu.VMEM((cx, cy, nz), f32),
             pltpu.VMEM((cx, cy, nz), f32),
             pltpu.VMEM((chunks, devices, rows, nz), f32),
@@ -397,15 +403,17 @@
             pltpu.VMEM((cx * cy, nz), f32),
             pltpu.VMEM((steps, cy, nz), f32),
             pltpu.VMEM((steps, cy, nz), f32),
-            pltpu.VMEM((steps, cx, nz), f32),
-            pltpu.VMEM((steps, cx, nz), f32),
+            pltpu.VMEM((steps, cx, 1, nz), f32),
+            pltpu.VMEM((steps, cx, 1, nz), f32),
             pltpu.VMEM((steps, 2, cy, nz), f32),
-            pltpu.VMEM((steps, 2, cx, nz), f32),
+            pltpu.VMEM((steps + 1, 2, cx, 1, nz), f32),
             pltpu.VMEM((cy, nz), f32),
             pltpu.VMEM((cy, nz), f32),
-            pltpu.VMEM((cx, nz), f32),
-            pltpu.VMEM((cx, nz), f32),
-            pltpu.VMEM((2, cx, nz), f32),
+            pltpu.VMEM((cx, 1, nz), f32),
+            pltpu.VMEM((cx, 1, nz), f32),
+            pltpu.VMEM((cy, nz), f32),
+            pltpu.VMEM((2, cx, 1, nz), f32),
+            dma((5,)),
             dma((chunks,)),
             dma((chunks,)),
             dma((2,)),

time: 102 us -> 79.1 us (0.78)
  Pallas kernels: 88.7 us -> 65.7 us
    pallas_call x1, Pallas kernels: 84 us -> 61 us  [per_device(): pl.pallas_call(functools.partial(wave_kernel, plan), out_shape=(field,) *...]
where the time goes in v2:
time: 79.1 us; the launch traced here: 78.7 us
  Pallas kernels  65.7 us (83%)
  local copies, waits for them, and re-layouts  12.3 us (16%)
    pallas_call x1, Pallas kernels, per_device(): pl.pallas_call(functools.partial(wave_kernel, plan), out_shape=(field,) *...  61 us
    unnamed x24, local copies, waits for them, and re-layouts  12.3 us
    pallas_call x1, Pallas kernels, per_device(): pl.pallas_call(functools.partial(pack_kernel, plan), out_shape=(jax.Shape...  4.71 us

profile of v2, /device:TPU:0, one launch (start us, length us, event | category | flops | bytes accessed | tf_op | source)
XLA Modules:
  0.0 78.7 jit_solution(3332933101831344677)
XLA Ops:
  0.6 0.0 copy-start
  0.6 1.2 %copy-done = f32[2,128,8,128]{3,2,1,0:T(8,128)S(1)} copy-done((f32[2,128,8,128]{3,2,1,0:T(8,128)S(1)}, f32[2,128,8,128]{3,2,1,0:T(8,128)}, u32[]{:S(2)}) %copy-start) | copy-done | bytes 1048600
  1.9 0.0 copy-start.6
  1.9 0.7 copy-done.6
  2.5 0.0 copy-start.7
  2.5 0.7 copy-done.7
  3.2 4.7 %pack.1 = (f32[8,32,16,128]{3,2,1,0:T(8,128)S(1)}, f32[32,1,128]{2,1,0:T(1,128)S(1)}) custom-call(s32[256]{0:T(256)S(1)} %bitcast.3, s32[2,128]{1,0:T(2,128)S(1)} %copy-done.7, f32[256,8,128]{2,1,0:T(8,128)S(1)} %bitcast.2), custom_call_target="tpu_custom_call" | custom-call | tf_op jit(solution)/shard_map/pack/pallas_call | solution.py:376
  7.9 0.0 copy-start.1
  8.0 1.0 %copy-done.1 = f32[32,32,128]{2,1,0:T(8,128)S(1)} copy-done((f32[32,32,128]{2,1,0:T(8,128)S(1)}, f32[32,32,128]{2,1,0:T(8,128)}, u32[]{:S(2)}) %copy-start.1) | copy-done | bytes 524312
  9.0 0.0 copy-start.2
  9.0 1.0 %copy-done.2 = f32[32,32,128]{2,1,0:T(8,128)S(1)} copy-done((f32[32,32,128]{2,1,0:T(8,128)S(1)}, f32[32,32,128]{2,1,0:T(8,128)}, u32[]{:S(2)}) %copy-start.2) | copy-done | bytes 524312
  10.0 0.0 copy-start.3
  10.0 1.0 %copy-done.3 = f32[32,32,128]{2,1,0:T(8,128)S(1)} copy-done((f32[32,32,128]{2,1,0:T(8,128)S(1)}, f32[32,32,128]{2,1,0:T(8,128)}, u32[]{:S(2)}) %copy-start.3) | copy-done | bytes 524312
  11.1 0.0 copy-start.4
  11.1 1.0 %copy-done.4 = f32[32,32,128]{2,1,0:T(8,128)S(1)} copy-done((f32[32,32,128]{2,1,0:T(8,128)S(1)}, f32[32,32,128]{2,1,0:T(8,128)}, u32[]{:S(2)}) %copy-start.4) | copy-done | bytes 524312
  12.1 0.0 copy-start.5
  12.1 1.0 %copy-done.5 = s32[32,32,128]{2,1,0:T(8,128)S(1)} copy-done((s32[32,32,128]{2,1,0:T(8,128)S(1)}, s32[32,32,128]{2,1,0:T(8,128)}, u32[]{:S(2)}) %copy-start.5) | copy-done | bytes 524312
  13.2 0.0 copy-start.8
  13.2 0.7 copy-done.8
  13.8 0.0 copy-start.9
  13.8 0.7 copy-done.9
  14.5 61.0 %wave.1 = (f32[32,32,128]{2,1,0:T(8,128)S(1)}, f32[32,32,128]{2,1,0:T(8,128)S(1)}, f32[32,32,128]{2,1,0:T(8,128)S(1)}, f32[32,32,128]{2,1,0:T(8,128)S(1)}) custom-call(f32[32,32,128]{2,1,0:T(8,128)S(1)} %copy-done.1, f32[32,32,128]{2,1,0:T(8,128)S(1)} %copy-done.2, f32[32,32,128]{2,1,0:T(8,128)S(1)} %copy-done.3, f32[32,32,128]{2,1,0:T(8,128)S(1)} %copy-done.4, ...), custom_call_target="tpu_custom_call" | custom-call | tf_op jit(solution)/shard_map/wave/pallas_call | solution.py:390
  75.5 0.8 %copy.18 = f32[32,32,128]{2,1,0:T(8,128)} copy(f32[32,32,128]{2,1,0:T(8,128)S(1)} %get-tuple-element.12) | data formatting | bytes 1048576
  76.3 0.8 %copy.19 = f32[32,32,128]{2,1,0:T(8,128)} copy(f32[32,32,128]{2,1,0:T(8,128)S(1)} %get-tuple-element.13) | data formatting | bytes 1048576
  77.1 0.8 %copy.20 = f32[32,32,128]{2,1,0:T(8,128)} copy(f32[32,32,128]{2,1,0:T(8,128)S(1)} %get-tuple-element.14) | data formatting | bytes 1048576
  77.9 0.8 %copy.21 = f32[32,32,128]{2,1,0:T(8,128)} copy(f32[32,32,128]{2,1,0:T(8,128)S(1)} %get-tuple-element.15) | data formatting | bytes 1048576
Async XLA Ops:
  0.6 1.2 %copy-start = (f32[2,128,8,128]{3,2,1,0:T(8,128)S(1)}, f32[2,128,8,128]{3,2,1,0:T(8,128)}, u32[]{:S(2)}) copy-start(f32[2,128,8,128]{3,2,1,0:T(8,128)} %param.17) | copy-start | bytes 3145732
  1.9 0.7 copy-start.6
  2.5 0.7 copy-start.7
  7.9 1.0 %copy-start.1 = (f32[32,32,128]{2,1,0:T(8,128)S(1)}, f32[32,32,128]{2,1,0:T(8,128)}, u32[]{:S(2)}) copy-start(f32[32,32,128]{2,1,0:T(8,128)} %p_in.1) | copy-start | bytes 1572868
  9.0 1.0 %copy-start.2 = (f32[32,32,128]{2,1,0:T(8,128)S(1)}, f32[32,32,128]{2,1,0:T(8,128)}, u32[]{:S(2)}) copy-start(f32[32,32,128]{2,1,0:T(8,128)} %vx_in.1) | copy-start | bytes 1572868
  10.0 1.0 %copy-start.3 = (f32[32,32,128]{2,1,0:T(8,128)S(1)}, f32[32,32,128]{2,1,0:T(8,128)}, u32[]{:S(2)}) copy-start(f32[32,32,128]{2,1,0:T(8,128)} %vy_in.1) | copy-start | bytes 1572868
  11.1 1.0 %copy-start.4 = (f32[32,32,128]{2,1,0:T(8,128)S(1)}, f32[32,32,128]{2,1,0:T(8,128)}, u32[]{:S(2)}) copy-start(f32[32,32,128]{2,1,0:T(8,128)} %vz_in.1) | copy-start | bytes 1572868
  12.1 1.0 %copy-start.5 = (s32[32,32,128]{2,1,0:T(8,128)S(1)}, s32[32,32,128]{2,1,0:T(8,128)}, u32[]{:S(2)}) copy-start(s32[32,32,128]{2,1,0:T(8,128)} %mat_in.1) | copy-start | bytes 1572868
  13.2 0.7 copy-start.8
  13.8 0.7 copy-start.9

commit v3 on v2

--- a/solution.py
+++ b/solution.py
@@ -21,14 +21,14 @@
     base = lax.rem(me, group) * rows
     lane = lax.broadcasted_iota(jnp.int32, (1, LANES), 1)
 
-    @pl.loop(0, devices)
+    @pl.loop(0, devices, unroll=4)
     def _(d):
         count_ref[d] = 0
         head_ref[d] = jnp.zeros((1, LANES), jnp.float32)
         for c in range(steps // per_chunk):
             out_ref[c, d] = jnp.zeros((rows, layers), jnp.float32)
 
-    @pl.loop(0, columns)
+    @pl.loop(0, columns, unroll=8)
     def _(c):
         t = tile_ref[c]
         slot = count_ref[t]

time: 79.1 us -> 77.7 us (0.982)
  Pallas kernels: 65.7 us -> 64.3 us
    pallas_call x1, Pallas kernels: 4.71 us -> 3.3 us  [per_device(): pl.pallas_call(functools.partial(pack_kernel, plan), out_shape=(jax.Shape...]
where the time goes in v3:
time: 77.7 us; the launch traced here: 77.3 us
  Pallas kernels  64.3 us (83%)
  local copies, waits for them, and re-layouts  12.3 us (16%)
    pallas_call x1, Pallas kernels, per_device(): pl.pallas_call(functools.partial(wave_kernel, plan), out_shape=(field,) *...  61 us
    unnamed x24, local copies, waits for them, and re-layouts  12.3 us
    pallas_call x1, Pallas kernels, per_device(): pl.pallas_call(functools.partial(pack_kernel, plan), out_shape=(jax.Shape...  3.3 us

profile of v3, /device:TPU:0, one launch (start us, length us, event | category | flops | bytes accessed | tf_op | source)
XLA Modules:
  0.0 77.3 jit_solution(11784119541285643006)
XLA Ops:
  0.6 0.0 copy-start
  0.6 1.2 %copy-done = f32[2,128,8,128]{3,2,1,0:T(8,128)S(1)} copy-done((f32[2,128,8,128]{3,2,1,0:T(8,128)S(1)}, f32[2,128,8,128]{3,2,1,0:T(8,128)}, u32[]{:S(2)}) %copy-start) | copy-done | bytes 1048600
  1.9 0.0 copy-start.6
  1.9 0.7 copy-done.6
  2.5 0.0 copy-start.7
  2.5 0.7 copy-done.7
  3.2 3.3 %pack.1 = (f32[8,32,16,128]{3,2,1,0:T(8,128)S(1)}, f32[32,1,128]{2,1,0:T(1,128)S(1)}) custom-call(s32[256]{0:T(256)S(1)} %bitcast.3, s32[2,128]{1,0:T(2,128)S(1)} %copy-done.7, f32[256,8,128]{2,1,0:T(8,128)S(1)} %bitcast.2), custom_call_target="tpu_custom_call" | custom-call | tf_op jit(solution)/shard_map/pack/pallas_call | solution.py:376
  6.5 0.0 copy-start.1
  6.5 1.0 %copy-done.1 = f32[32,32,128]{2,1,0:T(8,128)S(1)} copy-done((f32[32,32,128]{2,1,0:T(8,128)S(1)}, f32[32,32,128]{2,1,0:T(8,128)}, u32[]{:S(2)}) %copy-start.1) | copy-done | bytes 524312
  7.6 0.0 copy-start.2
  7.6 1.0 %copy-done.2 = f32[32,32,128]{2,1,0:T(8,128)S(1)} copy-done((f32[32,32,128]{2,1,0:T(8,128)S(1)}, f32[32,32,128]{2,1,0:T(8,128)}, u32[]{:S(2)}) %copy-start.2) | copy-done | bytes 524312
  8.6 0.0 copy-start.3
  8.6 1.0 %copy-done.3 = f32[32,32,128]{2,1,0:T(8,128)S(1)} copy-done((f32[32,32,128]{2,1,0:T(8,128)S(1)}, f32[32,32,128]{2,1,0:T(8,128)}, u32[]{:S(2)}) %copy-start.3) | copy-done | bytes 524312
  9.7 0.0 copy-start.4
  9.7 1.0 %copy-done.4 = f32[32,32,128]{2,1,0:T(8,128)S(1)} copy-done((f32[32,32,128]{2,1,0:T(8,128)S(1)}, f32[32,32,128]{2,1,0:T(8,128)}, u32[]{:S(2)}) %copy-start.4) | copy-done | bytes 524312
  10.7 0.0 copy-start.5
  10.7 1.0 %copy-done.5 = s32[32,32,128]{2,1,0:T(8,128)S(1)} copy-done((s32[32,32,128]{2,1,0:T(8,128)S(1)}, s32[32,32,128]{2,1,0:T(8,128)}, u32[]{:S(2)}) %copy-start.5) | copy-done | bytes 524312
  11.7 0.0 copy-start.8
  11.7 0.7 copy-done.8
  12.4 0.0 copy-start.9
  12.4 0.7 copy-done.9
  13.1 61.0 %wave.1 = (f32[32,32,128]{2,1,0:T(8,128)S(1)}, f32[32,32,128]{2,1,0:T(8,128)S(1)}, f32[32,32,128]{2,1,0:T(8,128)S(1)}, f32[32,32,128]{2,1,0:T(8,128)S(1)}) custom-call(f32[32,32,128]{2,1,0:T(8,128)S(1)} %copy-done.1, f32[32,32,128]{2,1,0:T(8,128)S(1)} %copy-done.2, f32[32,32,128]{2,1,0:T(8,128)S(1)} %copy-done.3, f32[32,32,128]{2,1,0:T(8,128)S(1)} %copy-done.4, ...), custom_call_target="tpu_custom_call" | custom-call | tf_op jit(solution)/shard_map/wave/pallas_call | solution.py:390
  74.1 0.8 %copy.18 = f32[32,32,128]{2,1,0:T(8,128)} copy(f32[32,32,128]{2,1,0:T(8,128)S(1)} %get-tuple-element.12) | data formatting | bytes 1048576
  74.9 0.8 %copy.19 = f32[32,32,128]{2,1,0:T(8,128)} copy(f32[32,32,128]{2,1,0:T(8,128)S(1)} %get-tuple-element.13) | data formatting | bytes 1048576
  75.7 0.8 %copy.20 = f32[32,32,128]{2,1,0:T(8,128)} copy(f32[32,32,128]{2,1,0:T(8,128)S(1)} %get-tuple-element.14) | data formatting | bytes 1048576
  76.5 0.8 %copy.21 = f32[32,32,128]{2,1,0:T(8,128)} copy(f32[32,32,128]{2,1,0:T(8,128)S(1)} %get-tuple-element.15) | data formatting | bytes 1048576
Async XLA Ops:
  0.6 1.2 %copy-start = (f32[2,128,8,128]{3,2,1,0:T(8,128)S(1)}, f32[2,128,8,128]{3,2,1,0:T(8,128)}, u32[]{:S(2)}) copy-start(f32[2,128,8,128]{3,2,1,0:T(8,128)} %param.17) | copy-start | bytes 3145732
  1.9 0.7 copy-start.6
  2.5 0.7 copy-start.7
  6.5 1.0 %copy-start.1 = (f32[32,32,128]{2,1,0:T(8,128)S(1)}, f32[32,32,128]{2,1,0:T(8,128)}, u32[]{:S(2)}) copy-start(f32[32,32,128]{2,1,0:T(8,128)} %p_in.1) | copy-start | bytes 1572868
  7.6 1.0 %copy-start.2 = (f32[32,32,128]{2,1,0:T(8,128)S(1)}, f32[32,32,128]{2,1,0:T(8,128)}, u32[]{:S(2)}) copy-start(f32[32,32,128]{2,1,0:T(8,128)} %vx_in.1) | copy-start | bytes 1572868
  8.6 1.0 %copy-start.3 = (f32[32,32,128]{2,1,0:T(8,128)S(1)}, f32[32,32,128]{2,1,0:T(8,128)}, u32[]{:S(2)}) copy-start(f32[32,32,128]{2,1,0:T(8,128)} %vy_in.1) | copy-start | bytes 1572868
  9.7 1.0 %copy-start.4 = (f32[32,32,128]{2,1,0:T(8,128)S(1)}, f32[32,32,128]{2,1,0:T(8,128)}, u32[]{:S(2)}) copy-start(f32[32,32,128]{2,1,0:T(8,128)} %vz_in.1) | copy-start | bytes 1572868
  10.7 1.0 %copy-start.5 = (s32[32,32,128]{2,1,0:T(8,128)S(1)}, s32[32,32,128]{2,1,0:T(8,128)}, u32[]{:S(2)}) copy-start(s32[32,32,128]{2,1,0:T(8,128)} %mat_in.1) | copy-start | bytes 1572868
  11.7 0.7 copy-start.8
  12.4 0.7 copy-start.9
